TPU v7x, 128 devices: a whole 4x4x4 slice. The times are simulated.
128 devices in a mesh: chan: 8 (over x, core), bl: 16 (over y, z).
Axes of the slice: x: 4, y: 4, z: 4, core: 2. Of those that a mesh axis runs over, the one named last changes fastest.
Arguments:
- visibilities: float32 [2, 128, 32768], P(None, 'chan', 'bl'), may hold values from -6 to 6
- coherencies: float32 [2, 8, 128, 32768], P(None, None, 'chan', 'bl'), may hold values from -0.5 to 0.5
- station_pairs: int32 [2, 32768], P(None, 'bl'), may hold values from 0 to 511, as said below
- gains_start: float32 [512, 2, 8, 128], P('bl', None, None, 'chan'), may hold values from -4 to 4
- consensus_prev: float32 [512, 2, 8, 128], P('bl', None, None, 'chan'), may hold values from -4 to 4
- dual_prev: float32 [512, 2, 8, 128], P('bl', None, None, 'chan'), may hold values from -4 to 4
- penalty: float32 [8], replicated, may hold values from 0.5 to 4
Outputs:
- gains: float32 [512, 2, 8, 128], P('bl', None, None, 'chan')
- consensus: float32 [512, 2, 8, 128], P('bl', None, None, 'chan')
- dual: float32 [512, 2, 8, 128], P('bl', None, None, 'chan')
Inputs may be any that keep to these rules, and one draw needn't show every extreme that they name: `station_pairs`: column b names the two stations of baseline b, the first below the second; no pair appears twice.
All inputs are finite; a program needn't handle non-finite values.
Results may differ from a plain program's by a relative error of at most 0.0003.
Values sent between devices are 32-bit elements; how exact they have to be, the bound alone decides.
No kernel may reach another device: no remote copies, remote signals or barrier semaphores. Data moves between devices by JAX's collectives and lax.ppermute only.
A program may use at most 64 MiB of HBM per device.

v0:
```python
import jax
import jax.numpy as jnp
from jax import lax
from jax.sharding import PartitionSpec as P

PASSES = 2
POLY = 4


def poly_basis(count, order):
    freq = 2.0 * (jnp.arange(count).astype(jnp.float32) + 0.5) / count - 1.0
    columns = []
    for power in range(order):
        vector = freq**power
        for before in columns:
            vector = vector - jnp.sum(before * vector) * before
        vector = vector / jnp.sqrt(jnp.sum(vector * vector))
        columns.append(vector)
    return jnp.stack(columns, axis=1)


def split_terms(terms):
    upper = lax.optimization_barrier(terms.astype(jnp.bfloat16))
    lower = (terms - upper.astype(jnp.float32)).astype(jnp.bfloat16)
    return (upper, lower)


def collect(onehot, parts):
    dims = (((1,), (1,)), ((), ()))
    total = lax.dot_general(onehot, parts[0], dims, preferred_element_type=jnp.float32)
    return total + lax.dot_general(onehot, parts[1], dims, preferred_element_type=jnp.float32)


def local_terms(visibilities, coherencies, gain_p, gain_q):
    coh_re, coh_im = (coherencies[0], coherencies[1])
    far_re = coh_re * gain_q[0] + coh_im * gain_q[1]
    far_im = coh_im * gain_q[0] - coh_re * gain_q[1]
    model_re = gain_p[0] * far_re - gain_p[1] * far_im
    model_im = gain_p[0] * far_im + gain_p[1] * far_re
    resid_re = visibilities[0] - jnp.sum(model_re, axis=0)
    resid_im = visibilities[1] - jnp.sum(model_im, axis=0)
    rest_re = resid_re[None] + model_re
    rest_im = resid_im[None] + model_im
    near_re = coh_re * gain_p[0] - coh_im * gain_p[1]
    near_im = coh_re * gain_p[1] + coh_im * gain_p[0]
    side_p = jnp.stack(
        [
            far_re * rest_re + far_im * rest_im,
            far_re * rest_im - far_im * rest_re,
            far_re * far_re + far_im * far_im,
        ]
    )
    side_q = jnp.stack(
        [
            near_re * rest_re + near_im * rest_im,
            near_im * rest_re - near_re * rest_im,
            near_re * near_re + near_im * near_im,
        ]
    )
    lanes = visibilities.shape[2]
    return (split_terms(side_p.reshape(-1, lanes)), split_terms(side_q.reshape(-1, lanes)))


def update(totals, cons_part, dual_part, mu_dir):
    mu_b = mu_dir[None, :, None]
    denom = totals[:, 2] + mu_b
    new_re = (totals[:, 0] + mu_b * cons_part[:, 0] - 0.5 * dual_part[:, 0]) / denom
    new_im = (totals[:, 1] + mu_b * cons_part[:, 1] - 0.5 * dual_part[:, 1]) / denom
    return jnp.stack([new_re, new_im], axis=1)


def local(
    visibilities, coherencies, station_pairs, gains_start, consensus_prev, dual_prev, penalty
):
    owned = gains_start.shape[0]
    chans = visibilities.shape[1]
    lanes = visibilities.shape[2]
    directions = coherencies.shape[1]
    stations = owned * lax.axis_size("bl")
    width = 2 * directions * chans
    first = station_pairs[0]
    second = station_pairs[1]
    labels = jnp.arange(stations, dtype=jnp.int32)[:, None]
    onehot_p = (labels == first[None, :]).astype(jnp.bfloat16)
    onehot_q = (labels == second[None, :]).astype(jnp.bfloat16)
    mu_dir = 0.5 * penalty
    gain_all, cons_all, dual_all = (
        lax.all_gather(gains_start, "bl", axis=0, tiled=True),
        lax.all_gather(consensus_prev, "bl", axis=0, tiled=True),
        lax.all_gather(dual_prev, "bl", axis=0, tiled=True),
    )
    for gain_pass in range(PASSES):
        table = gain_all.reshape(stations, width).T
        flat_p = jnp.take(table, first, axis=1)
        flat_q = jnp.take(table, second, axis=1)
        terms_p, terms_q = local_terms(
            visibilities,
            coherencies,
            flat_p.reshape(2, directions, chans, lanes),
            flat_q.reshape(2, directions, chans, lanes),
        )
        totals = lax.psum(collect(onehot_p, terms_p) + collect(onehot_q, terms_q), "bl")
        gain_all = update(
            totals.reshape(stations, 3, directions, chans), cons_all, dual_all, mu_dir
        )
    gain_own = lax.dynamic_slice_in_dim(gain_all, lax.axis_index("bl") * owned, owned, 0)
    basis = poly_basis(chans * lax.axis_size("chan"), POLY)
    mine = lax.dynamic_slice_in_dim(basis, lax.axis_index("chan") * chans, chans, 0)
    rho_b = penalty[None, None, :, None]
    target = gain_own + dual_prev / rho_b
    whole = lax.all_gather(target, "chan", axis=3, tiled=True)
    coef = jnp.einsum("sjkc,cm->sjkm", whole, basis, precision=lax.Precision.HIGHEST)
    consensus = jnp.einsum("sjkm,cm->sjkc", coef, mine, precision=lax.Precision.HIGHEST)
    dual = dual_prev + rho_b * (gain_own - consensus)
    return (gain_own, consensus, dual)


def solution(mesh):
    placed = (
        P(None, "chan", "bl"),
        P(None, None, "chan", "bl"),
        P(None, "bl"),
        P("bl", None, None, "chan"),
        P("bl", None, None, "chan"),
        P("bl", None, None, "chan"),
        P(),
    )
    return jax.shard_map(
        local,
        mesh=mesh,
        in_specs=placed,
        out_specs=(
            P("bl", None, None, "chan"),
            P("bl", None, None, "chan"),
            P("bl", None, None, "chan"),
        ),
        check_vma=False,
    )
```

profile of v0, /device:TPU:1, one launch (start us, length us, event | category | flops | bytes accessed | tf_op | source)
XLA Modules:
  0.0 340.9 jit_solution(3522280612685450564)
XLA Ops:
  9.2 33.2 %all_gather.12 = f32[512,2,8,16]{3,2,1,0:T(8,128)} all-gather(f32[32,2,8,16]{3,2,1,0:T(8,128)S(1)} %copy.70), channel_id=1, replica_groups=mesh['chan'=8,'bl'=16] {'bl'}, dimensions={0}, use_global_device_ids=true | all-gather | bytes 557056 | tf_op jit(solution)/shard_map/all_gather | solution.py:88
  42.4 2.8 copy.71
  45.4 8.6 %gather_fusion.1 = f32[2048,256]{1,0:T(8,128)} fusion(f32[256,512]{0,1:T(8,128)S(1)} %bitcast.125, s32[2048]{0:T(1024)S(1)} %fusion.43), kind=kCustom, calls=%fused_computation.1.clone | custom fusion | bytes 4202496 | tf_op jit(solution)/shard_map/jit(_take)/gather | solution.py:94
  54.0 1.9 select_bitcast_fusion.2
  55.9 1.1 fusion.64
  57.0 1.6 copy.78
  58.6 1.3 copy.75
  59.9 8.6 %gather_fusion = f32[2048,256]{1,0:T(8,128)} fusion(f32[256,512]{0,1:T(8,128)S(1)} %bitcast.126, s32[2048]{0:T(1024)S(1)} %fusion.44), kind=kCustom, calls=%fused_computation.clone | custom fusion | bytes 4202496 | tf_op jit(solution)/shard_map/jit(_take)/gather | solution.py:95
  68.5 1.9 select_bitcast_fusion.3
  70.4 1.5 fusion.63
  71.9 2.7 copy.73
  74.6 2.6 copy.74
  77.2 2.0 fusion.27
  80.8 1.3 multiply_add_fusion.7
  88.2 2.0 fusion.25
  90.5 31.3 %all_gather.14 = f32[512,2,8,16]{3,2,1,0:T(8,128)S(1)} all-gather(f32[32,2,8,16]{3,2,1,0:T(8,128)S(1)} %copy.83), channel_id=1, replica_groups=mesh['chan'=8,'bl'=16] {'bl'}, dimensions={0}, use_global_device_ids=true | all-gather | bytes 557056 | tf_op jit(solution)/shard_map/all_gather | solution.py:90
  121.8 2.3 fusion.60
  124.1 2.2 copy.99
  126.4 24.8 %all_gather.13 = f32[512,2,8,16]{3,2,1,0:T(8,128)S(1)} all-gather(f32[32,2,8,16]{3,2,1,0:T(8,128)S(1)} %copy.81), channel_id=1, replica_groups=mesh['chan'=8,'bl'=16] {'bl'}, dimensions={0}, use_global_device_ids=true | all-gather | bytes 557056 | tf_op jit(solution)/shard_map/all_gather | solution.py:89
  151.2 2.3 fusion.59
  153.5 2.2 copy.98
  155.7 2.3 copy.101
  158.0 2.3 copy.100
  164.2 1.2 multiply_reduce_fusion.5
  166.0 13.2 %all-reduce.3.cloned.1.call-done = f32[512,3,8,16]{0,3,2,1:T(8,128)} async-done(((f32[512,3,8,16]{0,3,2,1:T(8,128)}), f32[512,3,8,16]{0,3,2,1:T(8,128)}) %all-reduce.3.cloned.1.call-update) | async-done | bytes 786448 | tf_op jit(solution)/shard_map/psum | solution.py:102
  179.2 1.3 fusion.37
  181.4 1.2 copy.87
  182.6 8.6 %gather_fusion.3 = f32[2048,256]{1,0:T(8,128)} fusion(f32[256,512]{0,1:T(8,128)S(1)} %bitcast.127, s32[2048]{0:T(1024)S(1)} %fusion.43), kind=kCustom, calls=%fused_computation.3.clone | custom fusion | bytes 4202496 | tf_op jit(solution)/shard_map/jit(_take)/gather | solution.py:94
  191.2 8.6 %gather_fusion.2 = f32[2048,256]{1,0:T(8,128)} fusion(f32[256,512]{0,1:T(8,128)S(1)} %bitcast.128, s32[2048]{0:T(1024)S(1)} %fusion.44), kind=kCustom, calls=%fused_computation.2.clone | custom fusion | bytes 4202496 | tf_op jit(solution)/shard_map/jit(_take)/gather | solution.py:95
  199.8 1.9 select_bitcast_fusion
  201.7 1.5 fusion.62
  203.2 1.6 copy.93
  204.8 2.5 copy.90
  207.3 1.9 select_bitcast_fusion.1
  209.2 1.5 fusion.61
  210.7 2.5 copy.88
  213.2 2.6 copy.89
  215.8 2.0 fusion.29
  219.4 1.3 multiply_add_fusion.1
  223.8 1.1 fusion.21
  227.1 2.1 fusion.24
  230.5 1.3 multiply_reduce_fusion.2
  232.5 1.9 multiply_reduce_fusion.1
  234.4 1.9 multiply_reduce_fusion
  237.0 2.0 fusion.56
  239.1 75.6 %all-reduce.5.cloned.1.call-done = f32[512,3,8,16]{0,3,2,1:T(8,128)} async-done(((f32[512,3,8,16]{0,3,2,1:T(8,128)}), f32[512,3,8,16]{0,3,2,1:T(8,128)}) %all-reduce.5.cloned.1.call-update) | async-done | bytes 786448 | tf_op jit(solution)/shard_map/psum | solution.py:102
  314.7 1.3 fusion.33
  316.2 16.2 %all_gather.15 = f32[32,2,8,128]{0,3,2,1:T(8,128)S(1)} all-gather(f32[32,2,8,16]{0,3,2,1:T(8,128)S(1)} %get-tuple-element.17), channel_id=1, replica_groups=mesh['chan'=8,'bl'=16] {'chan'}, dimensions={3}, use_global_device_ids=true | all-gather | bytes 294912 | tf_op jit(solution)/shard_map/all_gather | solution.py:111
  (108 shorter events, 23.1 us)
Async XLA Ops:
  7.2 172.0 %all-reduce.3.cloned.1.call-start = ((), (), s32[]{:S(2)}) async-start(), calls=%async_computation | async-start | bytes 1572864 | tf_op jit(solution)/shard_map/psum | solution.py:102
  8.0 77.0 %copy-start.20 = (s32[1,2048]{1,0:T(1,128)}, s32[1,2048]{1,0:T(1,128)S(1)}, u32[]{:S(2)}) copy-start(s32[1,2048]{1,0:T(1,128)S(1)} %get-tuple-element.66) | copy-start | bytes 24580
  8.0 80.2 %copy-start.18 = (s32[1,2048]{1,0:T(1,128)}, s32[1,2048]{1,0:T(1,128)S(1)}, u32[]{:S(2)}) copy-start(s32[1,2048]{1,0:T(1,128)S(1)} %get-tuple-element.65) | copy-start | bytes 24580
  8.1 45.9 %copy-start.24 = (pred[2048]{0:T(1024)(128)(4,1)}, pred[2048]{0:T(1024)(128)(4,1)S(1)}, u32[]{:S(2)}) copy-start(pred[2048]{0:T(1024)(128)(4,1)S(1)} %compare_and_fusion.1) | copy-start | bytes 6148
  8.1 60.4 %copy-start.22 = (pred[2048]{0:T(1024)(128)(4,1)}, pred[2048]{0:T(1024)(128)(4,1)S(1)}, u32[]{:S(2)}) copy-start(pred[2048]{0:T(1024)(128)(4,1)S(1)} %compare_and_fusion) | copy-start | bytes 6148
  71.9 5.3 %copy-start = (f32[2,8,16,2048]{3,2,1,0:T(8,128)S(1)}, f32[2,8,16,2048]{3,2,1,0:T(8,128)}, u32[]{:S(2)}) copy-start(f32[2,8,16,2048]{3,2,1,0:T(8,128)} %param.10) | copy-start | bytes 6291460
  77.2 2.0 copy-start.1
  79.2 1.0 copy-start.14
  79.2 1.3 copy-start.3
  79.2 1.6 copy-start.5
  88.2 2.1 copy-start.13
  90.2 224.5 %all-reduce.5.cloned.1.call-start = ((), (), s32[]{:S(2)}) async-start(), calls=%async_computation.1 | async-start | bytes 1572864 | tf_op jit(solution)/shard_map/psum | solution.py:102
  124.1 2.2 copy-start.17
  155.7 23.5 %copy-start.7 = (f32[512,1,8,16]{0,3,2,1:T(8,128)}, f32[512,1,8,16]{0,3,2,1:T(8,128)S(1)}, u32[]{:S(2)}) copy-start(f32[512,1,8,16]{0,3,2,1:T(8,128)S(1)} %copy.98) | copy-start | bytes 786436
  155.7 9.7 %copy-start.28 = (f32[8]{0:T(128)S(1)}, f32[8]{0:T(128)}, u32[]{:S(2)}) copy-start(f32[8]{0:T(128)} %param.15) | copy-start | bytes 100
  158.0 22.5 %copy-start.9 = (f32[512,1,8,16]{0,3,2,1:T(8,128)}, f32[512,1,8,16]{0,3,2,1:T(8,128)S(1)}, u32[]{:S(2)}) copy-start(f32[512,1,8,16]{0,3,2,1:T(8,128)S(1)} %copy.101) | copy-start | bytes 786436
  160.2 22.4 %copy-start.11 = (f32[512,1,8,16]{0,3,2,1:T(8,128)}, f32[512,1,8,16]{0,3,2,1:T(8,128)S(1)}, u32[]{:S(2)}) copy-start(f32[512,1,8,16]{0,3,2,1:T(8,128)S(1)} %copy.100) | copy-start | bytes 786436
  191.2 8.6 %copy-start.25 = (pred[2048]{0:T(1024)(128)(4,1)S(1)}, pred[2048]{0:T(1024)(128)(4,1)}, u32[]{:S(2)}) copy-start(pred[2048]{0:T(1024)(128)(4,1)} %copy-done.24) | copy-start | bytes 6148
  203.2 4.1 %copy-start.23 = (pred[2048]{0:T(1024)(128)(4,1)S(1)}, pred[2048]{0:T(1024)(128)(4,1)}, u32[]{:S(2)}) copy-start(pred[2048]{0:T(1024)(128)(4,1)} %copy-done.22) | copy-start | bytes 6148
  215.8 2.0 copy-start.2
  217.8 1.0 copy-start.15
  217.8 1.3 copy-start.4
  217.8 1.6 copy-start.6
  222.0 0.7 copy-start.21
  225.3 0.7 copy-start.19
  227.1 3.4 copy-start.26
  227.1 87.6 %copy-start.8 = (f32[512,1,8,16]{0,3,2,1:T(8,128)S(1)}, f32[512,1,8,16]{0,3,2,1:T(8,128)}, u32[]{:S(2)}) copy-start(f32[512,1,8,16]{0,3,2,1:T(8,128)} %copy-done.7) | copy-start | bytes 786436
  227.1 87.6 %copy-start.10 = (f32[512,1,8,16]{0,3,2,1:T(8,128)S(1)}, f32[512,1,8,16]{0,3,2,1:T(8,128)}, u32[]{:S(2)}) copy-start(f32[512,1,8,16]{0,3,2,1:T(8,128)} %copy-done.9) | copy-start | bytes 786436
  227.1 87.6 %copy-start.12 = (f32[512,1,8,16]{0,3,2,1:T(8,128)S(1)}, f32[512,1,8,16]{0,3,2,1:T(8,128)}, u32[]{:S(2)}) copy-start(f32[512,1,8,16]{0,3,2,1:T(8,128)} %copy-done.11) | copy-start | bytes 786436
  227.1 87.6 %copy-start.27 = (f32[8]{0:T(128)S(1)}, f32[8]{0:T(128)}, u32[]{:S(2)}) copy-start(f32[8]{0:T(128)} %broadcast_multiply_fusion) | copy-start | bytes 100
  229.2 86.9 %copy-start.29 = (f32[8]{0:T(128)S(1)}, f32[8]{0:T(128)}, u32[]{:S(2)}) copy-start(f32[8]{0:T(128)} %param.15) | copy-start | bytes 100
  316.2 17.9 %copy-start.16 = (f32[32,2,8,16]{0,3,2,1:T(8,128)}, f32[32,2,8,16]{0,3,2,1:T(8,128)S(1)}, u32[]{:S(2)}) copy-start(f32[32,2,8,16]{0,3,2,1:T(8,128)S(1)} %get-tuple-element.18) | copy-start | bytes 98308
Sparse Core Ops, SparseCore 0:
  90.4 88.7 all-reduce.2
  229.3 85.3 all-reduce.4
where the time goes:
time: 342 us; the launch traced here: 341 us
  blocking collectives  105 us (31%)
  waiting for transfers between devices  88.8 us (26%)
  local copies, waits for them, and re-layouts  79.6 us (23%)
  other arithmetic  36.1 us (11%)
  between operations  18.7 us (5%)
  matrix products  12.3 us (4%)
    psum x2, waiting for transfers between devices, local(): lax.psum(collect(onehot_p, terms_p) + collect(onehot_q, terms_q), 'bl')  88.8 us
    all_gather x1, blocking collectives, local(): lax.all_gather(gains_start, 'bl', axis=0, tiled=True)  33.2 us
    all_gather x1, blocking collectives, local(): lax.all_gather(dual_prev, 'bl', axis=0, tiled=True)  31.3 us
    all_gather x1, blocking collectives, local(): lax.all_gather(consensus_prev, 'bl', axis=0, tiled=True)  24.8 us
    gather x2, local copies, waits for them, and re-layouts, local(): flat_q = jnp.take(table, second, axis=1)  17.2 us
    gather x2, local copies, waits for them, and re-layouts, local(): flat_p = jnp.take(table, first, axis=1)  17.2 us
    all_gather x1, blocking collectives, local(): whole = lax.all_gather(target, 'chan', axis=3, tiled=True)  16.2 us
    slice x6, local copies, waits for them, and re-layouts, local_terms(): far_re = coh_re * gain_q[0] + coh_im * gain_q[1]  13.3 us
  transfers between devices with their start and end apart: 2, of which 2 were waited for; matrix products, arithmetic and copies ran while one was open for 7% of the time, Pallas kernels for 0%

commit v1 on v0

v1 whole, which is shorter than its diff:
```python
import functools

import jax
import jax.numpy as jnp
import numpy as np
from jax import lax
from jax.experimental import pallas as pl
from jax.experimental.pallas import tpu as pltpu
from jax.sharding import PartitionSpec as P

PASSES = 2
POLY = 4
CHUNK = 256
VMEM = pl.BlockSpec(memory_space=pltpu.VMEM)
SMEM = pl.BlockSpec(memory_space=pltpu.SMEM)
LIMIT = pltpu.CompilerParams(vmem_limit_bytes=48 * 1024 * 1024)


def poly_basis(count, order):
    freq = 2.0 * (np.arange(count).astype(np.float64) + 0.5) / count - 1.0
    columns = []
    for power in range(order):
        vector = freq**power
        for before in columns:
            vector = vector - np.sum(before * vector) * before
        columns.append(vector / np.sqrt(np.sum(vector * vector)))
    return np.stack(columns, axis=1).astype(np.float32)


def spread(block, out_ref):
    for part in range(out_ref.shape[0]):
        out_ref[part] = block


def prep_kernel(gain_ref, out_ref):
    spread(gain_ref[...].T, out_ref)


def pass_kernel(dims, pairs_ref, table_ref, vis_ref, coh_ref, out_ref, table_scr, sums_scr):
    stations, directions, chans, lanes = dims
    rows = directions * chans
    width = 2 * rows
    flat = table_ref[...].reshape(stations, width).T
    upper = flat.astype(jnp.bfloat16)
    table_scr[0:width] = upper
    table_scr[width : 2 * width] = (flat - upper.astype(jnp.float32)).astype(jnp.bfloat16)
    labels = lax.broadcasted_iota(jnp.int32, (stations, CHUNK), 0)
    for chunk in range(lanes // CHUNK):
        cut = pl.ds(chunk * CHUNK, CHUNK)
        onehots = []
        gains = []
        for side in range(2):
            onehot = jnp.where(labels == pairs_ref[side : side + 1, cut], 1.0, 0.0)
            onehot = onehot.astype(jnp.bfloat16)
            both = jnp.dot(table_scr[...], onehot, preferred_element_type=jnp.float32)
            picked = both[0:width] + both[width : 2 * width]
            gains.append(picked.reshape(2, directions, chans, CHUNK))
            onehots.append(onehot)
        (gp_re, gp_im), (gq_re, gq_im) = gains
        coh_re = coh_ref[0, :, :, cut]
        coh_im = coh_ref[1, :, :, cut]
        cross_re = gp_re * gq_re + gp_im * gq_im
        cross_im = gp_im * gq_re - gp_re * gq_im
        model_re = coh_re * cross_re - coh_im * cross_im
        model_im = coh_re * cross_im + coh_im * cross_re
        res_re = (vis_ref[0, :, cut] - jnp.sum(model_re, axis=0))[None]
        res_im = (vis_ref[1, :, cut] - jnp.sum(model_im, axis=0))[None]
        turn_re = coh_re * res_re + coh_im * res_im
        turn_im = coh_re * res_im - coh_im * res_re
        power = coh_re * coh_re + coh_im * coh_im
        side_p = [
            turn_re * gq_re - turn_im * gq_im,
            turn_re * gq_im + turn_im * gq_re,
            power * (gq_re * gq_re + gq_im * gq_im),
        ]
        side_q = [
            turn_re * gp_re + turn_im * gp_im,
            turn_re * gp_im - turn_im * gp_re,
            power * (gp_re * gp_re + gp_im * gp_im),
        ]
        uppers = []
        lowers = []
        for terms in (side_p, side_q):
            whole = jnp.concatenate([t.reshape(rows, CHUNK) for t in terms], axis=0)
            upper = whole.astype(jnp.bfloat16)
            uppers.append(upper)
            lowers.append((whole - upper.astype(jnp.float32)).astype(jnp.bfloat16))
        terms = jnp.concatenate(
            [jnp.concatenate(uppers, axis=1), jnp.concatenate(lowers, axis=1)], axis=0
        )
        part = lax.dot_general(
            jnp.concatenate(onehots, axis=1),
            terms,
            (((1,), (1,)), ((), ())),
            preferred_element_type=jnp.float32,
        )
        if chunk == 0:
            sums_scr[...] = part
        else:
            sums_scr[...] += part
    out_ref[...] = (sums_scr[:, 0 : 3 * rows] + sums_scr[:, 3 * rows :]).reshape(out_ref.shape)


def per_lane(penalty_ref, directions, chans):
    lane = lax.broadcasted_iota(jnp.int32, (1, directions * chans), 1) // chans
    row = jnp.zeros((1, directions * chans), jnp.float32)
    for k in range(directions):
        row = jnp.where(lane == k, penalty_ref[k], row)
    return row


def solve(penalty_ref, sums_ref, gain_ref, cons_ref, dual_ref, directions, chans):
    rows = directions * chans
    mu = 0.5 * per_lane(penalty_ref, directions, chans)
    sums = jnp.sum(sums_ref[...], axis=0)
    cons = cons_ref[...].T
    dual = dual_ref[...].T
    power = sums[:, 2 * rows :]
    fresh = []
    for part in range(2):
        cut = slice(part * rows, (part + 1) * rows)
        top = sums[:, cut] + gain_ref[:, cut] * power + mu * cons[:, cut] - 0.5 * dual[:, cut]
        fresh.append(top / (power + mu))
    return jnp.concatenate(fresh, axis=1)


def update_kernel(dims, penalty_ref, sums_ref, gain_ref, cons_ref, dual_ref, out_ref):
    spread(solve(penalty_ref, sums_ref, gain_ref, cons_ref, dual_ref, *dims), out_ref)


def pack(block):
    depth = block.shape[0] * block.shape[1] // 128
    return jnp.concatenate(
        [block[first : first + depth] for first in range(0, block.shape[0], depth)], axis=1
    )


def unpack(block, lanes):
    return jnp.concatenate(
        [block[:, first : first + lanes] for first in range(0, 128, lanes)], axis=0
    )


def fit_kernel(
    dims, penalty_ref, basis_ref, sums_ref, gain_ref, cons_ref, dual_ref, gain_out, coef_ref
):
    directions, chans = dims
    gain = solve(penalty_ref, sums_ref, gain_ref, cons_ref, dual_ref, directions, chans).T
    gain_out[...] = gain
    coefs = []
    for part in range(2 * directions):
        cut = slice(part * chans, (part + 1) * chans)
        target = gain[cut] + dual_ref[cut] / penalty_ref[part % directions]
        for m in range(POLY):
            coefs.append(jnp.sum(target * basis_ref[:, m : m + 1], axis=0, keepdims=True))
    spread(pack(jnp.concatenate(coefs, axis=0)), coef_ref)


def finish_kernel(
    dims, penalty_ref, basis_ref, coef_ref, gain_ref, dual_ref, cons_out, dual_out
):
    directions, chans = dims
    coef = unpack(jnp.sum(coef_ref[...], axis=0), gain_ref.shape[1])
    for part in range(2 * directions):
        cut = slice(part * chans, (part + 1) * chans)
        cons = coef[part * POLY : part * POLY + 1] * basis_ref[:, 0:1]
        for m in range(1, POLY):
            cons += coef[part * POLY + m : part * POLY + m + 1] * basis_ref[:, m : m + 1]
        cons_out[cut] = cons
        dual_out[cut] = dual_ref[cut] + penalty_ref[part % directions] * (gain_ref[cut] - cons)


def local(
    visibilities, coherencies, station_pairs, gains_start, consensus_prev, dual_prev, penalty
):
    owned, _, directions, chans = gains_start.shape
    lanes = visibilities.shape[2]
    parts = lax.axis_size("bl")
    groups = lax.axis_size("chan")
    stations = owned * parts
    rows = directions * chans
    width = 2 * rows
    dims = (directions, chans)

    def flat(array):
        return jnp.transpose(array, (1, 2, 3, 0)).reshape(width, owned)

    def call(kernel, shapes, specs, **extra):
        return pl.pallas_call(
            kernel,
            out_shape=[jax.ShapeDtypeStruct(s, jnp.float32) for s in shapes],
            in_specs=specs,
            out_specs=[VMEM] * len(shapes),
            compiler_params=LIMIT,
            **extra,
        )

    gain_rows, cons_rows, dual_rows = flat(gains_start), flat(consensus_prev), flat(dual_prev)
    basis = jnp.asarray(poly_basis(chans * groups, POLY))
    mine = lax.dynamic_slice_in_dim(basis, lax.axis_index("chan") * chans, chans, 0)
    (copies,) = call(prep_kernel, [(parts, owned, width)], [VMEM])(gain_rows)
    for gain_pass in range(PASSES):
        table = lax.all_to_all(copies, "bl", 0, 0, tiled=True)
        (sums,) = call(
            functools.partial(pass_kernel, (stations, directions, chans, lanes)),
            [(parts, owned, 3 * rows)],
            [VMEM] * 4,
            scratch_shapes=[
                pltpu.VMEM((2 * width, stations), jnp.bfloat16),
                pltpu.VMEM((stations, 6 * rows), jnp.float32),
            ],
        )(station_pairs, table, visibilities, coherencies)
        sums = lax.all_to_all(sums, "bl", 0, 0, tiled=True)
        own = copies[0]
        if gain_pass < PASSES - 1:
            (copies,) = call(
                functools.partial(update_kernel, dims),
                [(parts, owned, width)],
                [SMEM] + [VMEM] * 4,
            )(penalty, sums, own, cons_rows, dual_rows)
    gain, coef = call(
        functools.partial(fit_kernel, dims),
        [(width, owned), (groups, 2 * directions * POLY * owned // 128, 128)],
        [SMEM] + [VMEM] * 5,
    )(penalty, mine, sums, own, cons_rows, dual_rows)
    coef = lax.all_to_all(coef, "chan", 0, 0, tiled=True)
    cons, dual = call(
        functools.partial(finish_kernel, dims),
        [(width, owned), (width, owned)],
        [SMEM] + [VMEM] * 4,
    )(penalty, mine, coef, gain, dual_rows)

    def back(array):
        return jnp.transpose(array.reshape(2, directions, chans, owned), (3, 0, 1, 2))

    return (back(gain), back(cons), back(dual))


def solution(mesh):
    placed = (
        P(None, "chan", "bl"),
        P(None, None, "chan", "bl"),
        P(None, "bl"),
        P("bl", None, None, "chan"),
        P("bl", None, None, "chan"),
        P("bl", None, None, "chan"),
        P(),
    )
    return jax.shard_map(
        local,
        mesh=mesh,
        in_specs=placed,
        out_specs=(
            P("bl", None, None, "chan"),
            P("bl", None, None, "chan"),
            P("bl", None, None, "chan"),
        ),
        check_vma=False,
    )
```

time: 342 us -> 108 us (0.32)
  local copies, waits for them, and re-layouts: 79.6 us -> 8.77 us
  waiting for transfers between devices: 88.8 us -> 21.4 us
  blocking collectives: 105 us -> 45.6 us
  other arithmetic: 36.1 us -> 0 us
  Pallas kernels: 0 us -> 23.3 us
  between operations: 18.7 us -> 0.71 us
  matrix products: 12.3 us -> 0 us
  starting transfers between devices: 0.08 us -> 7.36 us
    all_gather x4 -> x0, blocking collectives: 105 us -> none  [the longest x1 33.2 us: local(): lax.all_gather(gains_start, 'bl', axis=0, tiled=True)]
    psum x2 -> x0, waiting for transfers between devices: 88.8 us -> none  [local(): lax.psum(collect(onehot_p, terms_p) + collect(onehot_q, terms_q), 'bl')]
    all_to_all x0 -> x3, blocking collectives: none -> 45.6 us  [the longest x2 32.2 us: local(): table = lax.all_to_all(copies, 'bl', 0, 0, tiled=True)]
    gather x4 -> x0, local copies, waits for them, and re-layouts: 34.4 us -> none  [the longest x2 17.2 us: local(): flat_q = jnp.take(table, second, axis=1)]
    slice x15 -> x0, local copies, waits for them, and re-layouts: 28.3 us -> none  [the longest x6 13.3 us: local_terms(): far_re = coh_re * gain_q[0] + coh_im * gain_q[1]]
    pallas_call x0 -> x6, Pallas kernels: none -> 23.3 us  [the longest x2 19.6 us: local(): call(functools.partial(pass_kernel, (stations, directions, chans, lanes))...]
    all_to_all x0 -> x2, waiting for transfers between devices: none -> 21.4 us  [local(): sums = lax.all_to_all(sums, 'bl', 0, 0, tiled=True)]
    dot_general x10 -> x0, matrix products: 12.3 us -> none  [the longest x4 6.24 us: collect(): lax.dot_general(onehot, parts[0], dims, preferred_element_type=jnp.float32)]
  transfers between devices with their start and end apart: 2 -> 2, of which waited for: 2 -> 2; matrix products, arithmetic and copies ran while one was open for 7% -> 1% of each run, Pallas kernels for 0% -> 0%
where the time goes in v1:
time: 108 us; the launch traced here: 107 us
  blocking collectives  45.6 us (42%)
  Pallas kernels  23.3 us (22%)
  waiting for transfers between devices  21.4 us (20%)
  local copies, waits for them, and re-layouts  8.77 us (8%)
  starting transfers between devices  7.36 us (7%)
    all_to_all x2, blocking collectives, local(): table = lax.all_to_all(copies, 'bl', 0, 0, tiled=True)  32.2 us
    all_to_all x2, waiting for transfers between devices, local(): sums = lax.all_to_all(sums, 'bl', 0, 0, tiled=True)  21.4 us
    pallas_call x2, Pallas kernels, local(): call(functools.partial(pass_kernel, (stations, directions, chans, lanes))...  19.6 us
    all_to_all x1, blocking collectives, local(): coef = lax.all_to_all(coef, 'chan', 0, 0, tiled=True)  13.4 us
    unnamed x28, local copies, waits for them, and re-layouts  7.45 us
    all_to_all x2, starting transfers between devices, local(): sums = lax.all_to_all(sums, 'bl', 0, 0, tiled=True)  7.36 us
  transfers between devices with their start and end apart: 2, of which 2 were waited for; matrix products, arithmetic and copies ran while one was open for 1% of the time, Pallas kernels for 0%

profile of v1, /device:TPU:1, one launch (start us, length us, event | category | flops | bytes accessed | tf_op | source)
XLA Modules:
  0.0 107.1 jit_solution(4490819564696155022)
XLA Ops:
  0.6 0.0 copy-start.7
  0.6 0.9 copy-done.7
  1.5 0.1 shard_map.103
  1.7 18.7 %all_to_all.25.table_ref = f32[16,32,256]{2,1,0:T(8,128)S(1)} all-to-all(f32[16,32,256]{2,1,0:T(8,128)S(1)} %shard_map.103), channel_id=1, replica_groups=mesh['chan'=8,'bl'=16] {'bl'}, dimensions={0} | all-to-all | bytes 1048576 | tf_op jit(solution)/shard_map/all_to_all | solution.py:203
  20.4 0.0 copy-start
  20.4 1.6 %copy-done = f32[2,8,16,2048]{3,2,1,0:T(8,128)S(1)} copy-done((f32[2,8,16,2048]{3,2,1,0:T(8,128)S(1)}, f32[2,8,16,2048]{3,2,1,0:T(8,128)}, u32[]{:S(2)}) %copy-start) | copy-done | bytes 2097176
  21.9 0.0 copy-start.3
  21.9 0.9 copy-done.3
  22.9 0.0 copy-start.10
  22.9 0.7 copy-done.10
  23.6 0.0 copy-start.2
  23.6 0.0 copy-start.11
  23.6 9.8 %shard_map.104 = f32[16,32,384]{2,1,0:T(8,128)} custom-call(s32[2,2048]{1,0:T(2,128)S(1)} %copy-done.10, f32[16,32,256]{2,1,0:T(8,128)S(1)} %all_to_all.25.table_ref, f32[2,16,2048]{2,1,0:T(8,128)S(1)} %copy-done.3, f32[2,8,16,2048]{3,2,1,0:T(8,128)S(1)} %copy-done), custom_call_target="tpu_custom_call" | custom-call | tf_op jit(solution)/shard_map/pallas_call | solution.py:204
  33.4 0.0 copy-start.1
  33.4 3.7 %all-to-all-start.1 = ((f32[16,32,384]{2,1,0:T(8,128)}), f32[16,32,384]{2,1,0:T(8,128)S(1)}, u32[]{:S(2)}, u32[]{:S(2)}) async-start(f32[16,32,384]{2,1,0:T(8,128)} %shard_map.104), calls=%async_computation.1 | async-start | bytes 1572864 | tf_op jit(solution)/shard_map/all_to_all | solution.py:213
  37.2 0.6 slice_bitcast_fusion.1.gain_ref
  37.8 11.3 %all-to-all-done.1.sums_ref = f32[16,32,384]{2,1,0:T(8,128)S(1)} async-done(((f32[16,32,384]{2,1,0:T(8,128)}), f32[16,32,384]{2,1,0:T(8,128)S(1)}, u32[]{:S(2)}, u32[]{:S(2)}) %all-to-all-start.1) | async-done | bytes 786464 | tf_op jit(solution)/shard_map/all_to_all | solution.py:213
  49.1 0.0 copy-start.4
  49.1 0.0 copy-done.2
  49.1 0.0 copy-start.5
  49.1 0.9 copy-done.5
  50.0 0.0 copy-start.8
  50.0 0.8 copy-done.8
  50.8 0.0 copy-start.12
  50.8 0.7 copy-done.12
  51.5 0.7 shard_map.105
  52.2 13.5 %all_to_all.26.table_ref = f32[16,32,256]{2,1,0:T(8,128)S(1)} all-to-all(f32[16,32,256]{2,1,0:T(8,128)S(1)} %shard_map.105), channel_id=1, replica_groups=mesh['chan'=8,'bl'=16] {'bl'}, dimensions={0} | all-to-all | bytes 1048576 | tf_op jit(solution)/shard_map/all_to_all | solution.py:203
  65.7 0.0 copy-done.11
  65.7 0.0 copy-done.1
  65.7 0.0 copy-done.4
  65.7 0.0 copy-start.6
  65.7 0.0 copy-start.13
  65.7 9.8 %shard_map.106 = f32[16,32,384]{2,1,0:T(8,128)} custom-call(s32[2,2048]{1,0:T(2,128)S(1)} %copy-done.11, f32[16,32,256]{2,1,0:T(8,128)S(1)} %all_to_all.26.table_ref, f32[2,16,2048]{2,1,0:T(8,128)S(1)} %copy-done.4, f32[2,8,16,2048]{3,2,1,0:T(8,128)S(1)} %copy-done.1), custom_call_target="tpu_custom_call" | custom-call | tf_op jit(solution)/shard_map/pallas_call | solution.py:204
  75.5 3.6 %all-to-all-start.3 = ((f32[16,32,384]{2,1,0:T(8,128)}), f32[16,32,384]{2,1,0:T(8,128)S(1)}, u32[]{:S(2)}, u32[]{:S(2)}) async-start(f32[16,32,384]{2,1,0:T(8,128)} %shard_map.106), calls=%async_computation.3 | async-start | bytes 1572864 | tf_op jit(solution)/shard_map/all_to_all | solution.py:213
  79.1 0.7 constant_dynamic-slice_fusion.basis_ref
  79.8 10.1 %all-to-all-done.3.sums_ref = f32[16,32,384]{2,1,0:T(8,128)S(1)} async-done(((f32[16,32,384]{2,1,0:T(8,128)}), f32[16,32,384]{2,1,0:T(8,128)S(1)}, u32[]{:S(2)}, u32[]{:S(2)}) %all-to-all-start.3) | async-done | bytes 786464 | tf_op jit(solution)/shard_map/all_to_all | solution.py:213
  89.9 0.0 copy-done.6
  89.9 0.0 copy-done.13
  89.9 1.4 %shard_map.107 = (f32[256,32]{1,0:T(8,128)}, f32[8,16,128]{2,1,0:T(8,128)S(1)}) custom-call(f32[8]{0:T(128)S(1)} %copy-done.13, f32[16,4]{1,0:T(8,128)S(1)} %constant_dynamic-slice_fusion.basis_ref, f32[16,32,384]{2,1,0:T(8,128)S(1)} %all-to-all-done.3.sums_ref, f32[32,256]{1,0:T(8,128)S(1)} %slice_bitcast_fusion.gain_ref, f32[256,32]{1,0:T(8,128)S(1)} %bitcast.26, ...), custom_call_target="tpu_custom_call" | custom-call | tf_op jit(solution)/shard_map/pallas_call | solution.py:221
  91.3 13.4 %all_to_all.27.coef_ref = f32[8,16,128]{2,1,0:T(8,128)S(1)} all-to-all(f32[8,16,128]{2,1,0:T(8,128)S(1)} %get-tuple-element.8), channel_id=1, replica_groups=mesh['chan'=8,'bl'=16] {'chan'}, dimensions={0} | all-to-all | bytes 131072 | tf_op jit(solution)/shard_map/all_to_all | solution.py:226
  104.6 0.0 copy-start.9
  104.6 0.9 copy-done.9
  105.5 1.5 %shard_map.108 = (f32[256,32]{1,0:T(8,128)}, f32[256,32]{1,0:T(8,128)}) custom-call(f32[8]{0:T(128)S(1)} %copy-done.13, f32[16,4]{1,0:T(8,128)S(1)} %constant_dynamic-slice_fusion.basis_ref, f32[8,16,128]{2,1,0:T(8,128)S(1)} %all_to_all.27.coef_ref, f32[256,32]{1,0:T(8,128)S(1)} %copy-done.9, f32[256,32]{1,0:T(8,128)S(1)} %bitcast.24), custom_call_target="tpu_custom_call" | custom-call | tf_op jit(solution)/shard_map/pallas_call | solution.py:227
  (1 shorter events, 0.0 us)
Async XLA Ops:
  0.6 0.9 copy-start.7
  20.4 1.6 %copy-start = (f32[2,8,16,2048]{3,2,1,0:T(8,128)S(1)}, f32[2,8,16,2048]{3,2,1,0:T(8,128)}, u32[]{:S(2)}) copy-start(f32[2,8,16,2048]{3,2,1,0:T(8,128)} %coh_ref.3) | copy-start | bytes 6291460
  21.9 0.9 copy-start.3
  22.9 0.7 copy-start.10
  23.6 25.5 %copy-start.2 = (f32[32,2,8,16]{0,3,2,1:T(8,128)S(1)}, f32[32,2,8,16]{0,3,2,1:T(8,128)}, u32[]{:S(2)}) copy-start(f32[32,2,8,16]{0,3,2,1:T(8,128)} %param.13) | copy-start | bytes 98308
  23.6 42.0 %copy-start.11 = (s32[2,2048]{1,0:T(2,128)S(1)}, s32[2,2048]{1,0:T(2,128)}, u32[]{:S(2)}) copy-start(s32[2,2048]{1,0:T(2,128)} %pairs_ref.3) | copy-start | bytes 49156
  33.4 32.2 %copy-start.1 = (f32[2,8,16,2048]{3,2,1,0:T(8,128)S(1)}, f32[2,8,16,2048]{3,2,1,0:T(8,128)}, u32[]{:S(2)}) copy-start(f32[2,8,16,2048]{3,2,1,0:T(8,128)} %coh_ref.3) | copy-start | bytes 6291460
  33.4 15.7 %all-to-all-start.1 = ((f32[16,32,384]{2,1,0:T(8,128)}), f32[16,32,384]{2,1,0:T(8,128)S(1)}, u32[]{:S(2)}, u32[]{:S(2)}) async-start(f32[16,32,384]{2,1,0:T(8,128)} %shard_map.104), calls=%async_computation.1 | async-start | bytes 1572864 | tf_op jit(solution)/shard_map/all_to_all | solution.py:213
  49.1 16.6 %copy-start.4 = (f32[2,16,2048]{2,1,0:T(8,128)S(1)}, f32[2,16,2048]{2,1,0:T(8,128)}, u32[]{:S(2)}) copy-start(f32[2,16,2048]{2,1,0:T(8,128)} %vis_ref.3) | copy-start | bytes 786436
  49.1 0.9 copy-start.5
  50.0 0.8 copy-start.8
  50.8 0.7 copy-start.12
  65.7 24.2 %copy-start.6 = (f32[32,2,8,16]{0,3,2,1:T(8,128)S(1)}, f32[32,2,8,16]{0,3,2,1:T(8,128)}, u32[]{:S(2)}) copy-start(f32[32,2,8,16]{0,3,2,1:T(8,128)} %param.12) | copy-start | bytes 98308
  65.7 24.2 %copy-start.13 = (f32[8]{0:T(128)S(1)}, f32[8]{0:T(128)}, u32[]{:S(2)}) copy-start(f32[8]{0:T(128)} %penalty_ref.5) | copy-start | bytes 100
  75.5 14.4 %all-to-all-start.3 = ((f32[16,32,384]{2,1,0:T(8,128)}), f32[16,32,384]{2,1,0:T(8,128)S(1)}, u32[]{:S(2)}, u32[]{:S(2)}) async-start(f32[16,32,384]{2,1,0:T(8,128)} %shard_map.106), calls=%async_computation.3 | async-start | bytes 1572864 | tf_op jit(solution)/shard_map/all_to_all | solution.py:213
  104.6 0.9 copy-start.9

commit v2 on v0

v2 whole, which is shorter than its diff:
```python
import functools

import jax
import jax.numpy as jnp
import numpy as np
from jax import lax
from jax.experimental import pallas as pl
from jax.experimental.pallas import tpu as pltpu
from jax.sharding import PartitionSpec as P

PASSES = 2
POLY = 4
LANE = 128
GROUP = 1
UNROLL = 4
VMEM = pl.BlockSpec(memory_space=pltpu.VMEM)
SMEM = pl.BlockSpec(memory_space=pltpu.SMEM)
HBM = pl.BlockSpec(memory_space=pltpu.HBM)
LIMIT = pltpu.CompilerParams(vmem_limit_bytes=40 * 1024 * 1024)


def poly_basis(count, order):
    freq = 2.0 * (np.arange(count).astype(np.float64) + 0.5) / count - 1.0
    columns = []
    for power in range(order):
        vector = freq**power
        for before in columns:
            vector = vector - np.sum(before * vector) * before
        columns.append(vector / np.sqrt(np.sum(vector * vector)))
    return np.stack(columns, axis=1).astype(np.float32)


def prep_kernel(dims, vis_hbm, coh_hbm, pairs_hbm, *rest):
    directions, chans, start, tiles, owned, with_own = dims
    if with_own:
        gain_hbm, cons_hbm, dual_hbm, out_ref, coh_scr, vis_scr, pairs_scr, sems, own_scr, all_scr = rest
    else:
        out_ref, coh_scr, vis_scr, pairs_scr, sems = rest
    base = tiles * 2 * directions
    copies = [pltpu.make_async_copy(pairs_hbm, pairs_scr, sems.at[2 * tiles])]
    if with_own:
        for i, ref in enumerate((gain_hbm, cons_hbm, dual_hbm)):
            copies.append(pltpu.make_async_copy(ref, own_scr.at[i], sems.at[2 * tiles + 1 + i]))
    vis_copies = []
    coh_copies = []
    for tile in range(tiles):
        cut = pl.ds((start + tile) * LANE, LANE)
        coh_copies.append(
            pltpu.make_async_copy(coh_hbm.at[:, cut], coh_scr.at[tile], sems.at[tile])
        )
        vis_copies.append(
            pltpu.make_async_copy(
                vis_hbm.at[:, :, cut],
                vis_scr.at[:, pl.ds(tile * chans, chans)],
                sems.at[tiles + tile],
            )
        )
    for copy in copies + coh_copies + vis_copies:
        copy.start()
    for copy in copies:
        copy.wait()
    if with_own:
        own = [own_scr[i] for i in range(3)]
        all_scr[...] = jnp.concatenate(own + [jnp.zeros_like(own[0])], axis=1)
        for chan in range(chans):
            rows = pl.ds(chan, 2 * directions, stride=chans)
            out_ref[chan, pl.ds(base + 4 * tiles, 2 * directions)] = all_scr[rows, :]
    for tile in range(tiles):
        for side in range(2):
            row = pairs_scr[side : side + 1, pl.ds((start + tile) * LANE, LANE)]
            row = row.astype(jnp.float32)
            for chan in range(chans):
                out_ref[chan, pl.ds(base + (2 + side) * tiles + tile, 1)] = row
    for tile in range(tiles):
        coh_copies[tile].wait()
        for chan in range(chans):
            for part in range(2):
                out_ref[chan, pl.ds((2 * tile + part) * directions, directions)] = coh_scr[
                    tile, pl.ds(part * directions * chans + chan, directions, stride=chans)
                ]
    for copy in vis_copies:
        copy.wait()
    for chan in range(chans):
        for part in range(2):
            out_ref[chan, pl.ds(base + part * tiles, tiles)] = vis_scr[
                part, pl.ds(chan, tiles, stride=chans)
            ]


def pick(tables, low, highs):
    out = None
    for index, table in enumerate(tables):
        found = jnp.take_along_axis(table, low, axis=1)
        out = found if index == 0 else jnp.where(highs[index], found, out)
    return out


def split_pack(re, im, power):
    pair = jnp.concatenate([re, im], axis=0)
    upper = pair.astype(jnp.bfloat16)
    lower = (pair - upper.astype(jnp.float32)).astype(jnp.bfloat16)
    rest = power - power.astype(jnp.bfloat16).astype(jnp.float32)
    last = jnp.concatenate([power, rest], axis=0).astype(jnp.bfloat16)
    return upper, lower, last


def per_direction(penalty_ref, shape, period):
    row = (lax.broadcasted_iota(jnp.int32, shape, 0) // period) % penalty_ref.shape[0]
    rho = jnp.zeros(shape, jnp.float32)
    for k in range(penalty_ref.shape[0]):
        rho = jnp.where(row == k, penalty_ref[k], rho)
    return rho


class Sweep:
    def __init__(self, dims, x_ref, pair_scr, sums_scr):
        self.directions, self.tiles, self.stations, self.parts = dims
        self.x_ref, self.pair_scr, self.sums_scr = x_ref, pair_scr, sums_scr
        self.first = self.tiles * 2 * self.directions

    def index(self):
        tiles = self.tiles
        for part in range(self.parts):
            whole = self.x_ref[part, pl.ds(self.first + 2 * tiles, 2 * tiles)].astype(jnp.int32)
            self.pair_scr[part, pl.ds(0, 2 * tiles)] = jnp.bitwise_and(whole, LANE - 1)
            self.pair_scr[part, pl.ds(2 * tiles, 2 * tiles)] = jnp.right_shift(whole, 7)

    def fill(self, part, tables):
        directions, tiles, first = self.directions, self.tiles, self.first
        x_ref, pair_scr = self.x_ref, self.pair_scr
        stripes = self.stations // LANE
        depth = 6 * directions
        wide = (LANE // 16, 16, LANE)
        labels = lax.broadcasted_iota(jnp.int32, (LANE, LANE), 0).astype(jnp.float32)
        labels = labels.astype(jnp.bfloat16).reshape(wide)
        one, zero = jnp.ones(wide, jnp.bfloat16), jnp.zeros(wide, jnp.bfloat16)

        def twice(rows):
            return jnp.concatenate([rows, rows], axis=0).astype(jnp.bfloat16)

        def rows16(row):
            return jnp.broadcast_to(row.astype(jnp.float32), (16, LANE)).astype(jnp.bfloat16)

        lefts, rights = [], []
        for tile in range(tiles):
            gains = []
            masks = []
            for side in range(2):
                low = pair_scr[part, pl.ds(side * tiles + tile, 1)]
                high = pair_scr[part, pl.ds((2 + side) * tiles + tile, 1)]
                low8 = jnp.broadcast_to(low, (directions, LANE))
                high8 = jnp.broadcast_to(high, (directions, LANE))
                highs = [high8 == s for s in range(stripes)]
                gains.append([pick(tables[j], low8, highs) for j in range(2)])
                masks.append([twice(jnp.where(h, 1.0, 0.0)) for h in highs])
                hot = jnp.where(labels == rows16(low)[None], one, zero)
                rights.append(hot.reshape(LANE, LANE))
            (gp_re, gp_im), (gq_re, gq_im) = gains
            coh_re, coh_im = [
                x_ref[part, pl.ds((2 * tile + j) * directions, directions)] for j in range(2)
            ]
            cross_re = gp_re * gq_re + gp_im * gq_im
            cross_im = gp_im * gq_re - gp_re * gq_im
            model_re = coh_re * cross_re - coh_im * cross_im
            model_im = coh_re * cross_im + coh_im * cross_re
            res_re = x_ref[part, pl.ds(first + tile, 1)] - jnp.sum(model_re, axis=0, keepdims=True)
            res_im = x_ref[part, pl.ds(first + tiles + tile, 1)] - jnp.sum(
                model_im, axis=0, keepdims=True
            )
            turn_re = coh_re * res_re + coh_im * res_im
            turn_im = coh_re * res_im - coh_im * res_re
            power = coh_re * coh_re + coh_im * coh_im
            terms_p = split_pack(
                turn_re * gq_re - turn_im * gq_im,
                turn_re * gq_im + turn_im * gq_re,
                power * (gq_re * gq_re + gq_im * gq_im),
            )
            terms_q = split_pack(
                turn_re * gp_re + turn_im * gp_im,
                turn_re * gp_im - turn_im * gp_re,
                power * (gp_re * gp_re + gp_im * gp_im),
            )
            for side, terms in enumerate((terms_p, terms_q)):
                both = jnp.stack(terms)
                lefts.append(
                    jnp.concatenate(
                        [
                            (both * masks[side][s][None]).reshape(depth, LANE)
                            for s in range(stripes)
                        ],
                        axis=0,
                    )
                )
            if (tile + 1) % GROUP == 0:
                self.sums_scr[...] += lax.dot_general(
                    jnp.concatenate(lefts, axis=1),
                    jnp.concatenate(rights, axis=1),
                    (((1,), (1,)), ((), ())),
                    preferred_element_type=jnp.float32,
                )
                lefts, rights = [], []

    def run(self, tables):
        @pl.loop(0, self.parts // UNROLL)
        def _(step):
            for i in range(UNROLL):
                self.fill(UNROLL * step + i, tables)


def read_tables(table_scr, stations):
    return [
        [table_scr[j, :, pl.ds(s * LANE, LANE)] for s in range(stations // LANE)]
        for j in range(2)
    ]


def own_rows(x_ref, at, owned, parts, directions):
    own = [x_ref[part, pl.ds(at, 2 * directions)] for part in range(parts)]
    return [
        jnp.concatenate([block[:, i * owned : (i + 1) * owned] for block in own], axis=1)
        for i in range(3)
    ]


def main_kernel(
    dims, owned, groups, penalty_ref, x_ref, out_ref, table_scr, base_scr, pair_scr, sums_scr
):
    directions, tiles, stations, parts = dims
    stripes = stations // LANE
    depth = 6 * directions
    rho = per_direction(penalty_ref, (directions, 1), 1)
    mu = 0.5 * rho

    gain, cons, dual = own_rows(x_ref, tiles * (2 * directions + 4), owned, parts, directions)
    for j in range(2):
        cut = slice(j * directions, (j + 1) * directions)
        table_scr[j] = gain[cut]
        base_scr[j] = mu * cons[cut] - 0.5 * dual[cut]
        base_scr[2 + j] = dual[cut] / rho
    sweep = Sweep(dims, x_ref, pair_scr, sums_scr)
    sweep.index()

    for gain_pass in range(PASSES):
        tables = read_tables(table_scr, stations)
        sums_scr[...] = jnp.zeros_like(sums_scr)
        sweep.run(tables)
        for s in range(stripes):
            cut = pl.ds(s * LANE, LANE)
            block = sums_scr[pl.ds(s * depth, depth)]
            total = block[0 : 2 * directions] + block[2 * directions : 4 * directions]
            power = block[4 * directions : 5 * directions] + block[5 * directions :]
            for j in range(2):
                top = total[j * directions : (j + 1) * directions]
                top = top + table_scr[j, :, cut] * power + base_scr[j, :, cut]
                table_scr[j, :, cut] = top / (power + mu)

    half = directions // 2
    for part in range(parts):
        cut = pl.ds(part * owned, owned)
        pieces = []
        for j in range(2):
            target = table_scr[j, :, cut] + base_scr[2 + j, :, cut]
            pieces += [target[0:half], target[half:]]
        block = jnp.concatenate(pieces, axis=1)
        for group in range(groups):
            out_ref[group * parts + part] = block


def finish_kernel(
    dims, penalty_ref, basis_ref, x_ref, dual_ref, gain_out, cons_out, dual_out, out_scr
):
    directions, chans, owned, count = dims
    half = directions // 2
    start = lax.axis_index("chan") * chans
    coefs = [jnp.zeros((half, LANE), jnp.float32) for _ in range(POLY)]
    for channel in range(count):
        block = x_ref[channel]
        for m in range(POLY):
            coefs[m] = coefs[m] + block * basis_ref[channel * POLY + m]
    for chan in range(chans):
        block = x_ref[start + chan]
        cons = coefs[0] * basis_ref[(start + chan) * POLY]
        for m in range(1, POLY):
            cons = cons + coefs[m] * basis_ref[(start + chan) * POLY + m]
        for j in range(2):
            rows = pl.ds(j * directions * chans + chan, directions, stride=chans)
            pieces = []
            for source in (block, cons):
                cuts = [source[:, (2 * j + h) * owned : (2 * j + h + 1) * owned] for h in range(2)]
                pieces.append(jnp.concatenate(cuts, axis=0))
            out_scr[rows, :] = jnp.concatenate(pieces + pieces, axis=1)
    whole = out_scr[...]
    rho = per_direction(penalty_ref, (2 * directions * chans, 1), chans)
    dual = dual_ref[...]
    gain = whole[:, 0:owned] - dual / rho
    cons = whole[:, owned : 2 * owned]
    gain_out[...] = gain
    cons_out[...] = cons
    dual_out[...] = dual + rho * (gain - cons)


def local(
    visibilities, coherencies, station_pairs, gains_start, consensus_prev, dual_prev, penalty
):
    owned, _, directions, chans = gains_start.shape
    lanes = visibilities.shape[2]
    parts = lax.axis_size("bl")
    groups = lax.axis_size("chan")
    stations = owned * parts
    tiles = lanes // LANE
    rows = directions * chans
    width = 2 * rows
    depth = 6 * directions * (stations // LANE)

    def flat(array):
        return jnp.transpose(array, (1, 2, 3, 0)).reshape(width, owned)

    def call(kernel, shapes, specs, limit=LIMIT, **extra):
        return pl.pallas_call(
            kernel,
            out_shape=[jax.ShapeDtypeStruct(s, jnp.float32) for s in shapes],
            in_specs=specs,
            out_specs=[VMEM] * len(shapes),
            compiler_params=limit,
            **extra,
        )

    own = (flat(gains_start), flat(consensus_prev), flat(dual_prev))
    basis = jnp.asarray(poly_basis(chans * groups, POLY).reshape(-1))

    def prep(start, span, own):
        count = span * (2 * directions + 4) + (2 * directions if own else 0)
        scratch = [
            pltpu.VMEM((span, width, LANE), jnp.float32),
            pltpu.VMEM((2, span * chans, LANE), jnp.float32),
            pltpu.VMEM(station_pairs.shape, jnp.int32),
            pltpu.SemaphoreType.DMA((2 * span + 4,)),
        ]
        if own:
            scratch.append(pltpu.VMEM((3, width, owned), jnp.float32))
            scratch.append(pltpu.VMEM((width, LANE), jnp.float32))
        dims = (directions, chans, start, span, owned, bool(own))
        return call(
            functools.partial(prep_kernel, dims),
            [(chans, count, LANE)],
            [HBM] * (3 + len(own)),
            limit=pltpu.CompilerParams(),
            scratch_shapes=scratch,
        )(visibilities, coherencies.reshape(width, lanes), station_pairs, *own)[0]

    x = lax.all_to_all(prep(0, tiles, own), "bl", 0, 0, tiled=True)
    dims = (directions, tiles, stations, parts)
    (sent,) = call(
        functools.partial(main_kernel, dims, owned, groups),
        [(groups * parts, directions // 2, LANE)],
        [SMEM, VMEM],
        scratch_shapes=[
            pltpu.VMEM((2, directions, stations), jnp.float32),
            pltpu.VMEM((4, directions, stations), jnp.float32),
            pltpu.VMEM((parts, 4 * tiles, LANE), jnp.int32),
            pltpu.VMEM((depth, LANE), jnp.float32),
        ],
    )(penalty, x)
    held = lax.all_to_all(sent, ("chan", "bl"), 0, 0, tiled=True)
    outs = call(
        functools.partial(finish_kernel, (directions, chans, owned, chans * groups)),
        [(width, owned)] * 3,
        [SMEM, SMEM, VMEM, VMEM],
        scratch_shapes=[pltpu.VMEM((width, LANE), jnp.float32)],
    )(penalty, basis, held, own[2])

    def back(array):
        return jnp.transpose(array.reshape(2, directions, chans, owned), (3, 0, 1, 2))

    return tuple(back(array) for array in outs)


def solution(mesh):
    placed = (
        P(None, "chan", "bl"),
        P(None, None, "chan", "bl"),
        P(None, "bl"),
        P("bl", None, None, "chan"),
        P("bl", None, None, "chan"),
        P("bl", None, None, "chan"),
        P(),
    )
    return jax.shard_map(
        local,
        mesh=mesh,
        in_specs=placed,
        out_specs=(
            P("bl", None, None, "chan"),
            P("bl", None, None, "chan"),
            P("bl", None, None, "chan"),
        ),
        check_vma=False,
    )
```

time: 342 us -> 88.2 us (0.26)
  waiting for transfers between devices: 88.8 us -> 0 us
  local copies, waits for them, and re-layouts: 79.6 us -> 0.01 us
  blocking collectives: 105 us -> 61.8 us
  other arithmetic: 36.1 us -> 0 us
  Pallas kernels: 0 us -> 25.6 us
  between operations: 18.7 us -> 0.66 us
  matrix products: 12.3 us -> 0 us
    all_gather x4 -> x0, blocking collectives: 105 us -> none  [the longest x1 33.2 us: local(): lax.all_gather(gains_start, 'bl', axis=0, tiled=True)]
    psum x2 -> x0, waiting for transfers between devices: 88.8 us -> none  [local(): lax.psum(collect(onehot_p, terms_p) + collect(onehot_q, terms_q), 'bl')]
    all_to_all x0 -> x2, blocking collectives: none -> 61.8 us  [the longest x1 43.1 us: local(): x = lax.all_to_all(prep(0, tiles, own), 'bl', 0, 0, tiled=True)]
    gather x4 -> x0, local copies, waits for them, and re-layouts: 34.4 us -> none  [the longest x2 17.2 us: local(): flat_q = jnp.take(table, second, axis=1)]
    slice x15 -> x0, local copies, waits for them, and re-layouts: 28.3 us -> none  [the longest x6 13.3 us: local_terms(): far_re = coh_re * gain_q[0] + coh_im * gain_q[1]]
    pallas_call x0 -> x3, Pallas kernels: none -> 25.6 us  [the longest x1 19.9 us: local(): call(functools.partial(main_kernel, dims, owned, groups), [(groups * part...]
    unnamed x67 -> x6, local copies, waits for them, and re-layouts: 12.8 us -> 0.01 us
    dot_general x10 -> x0, matrix products: 12.3 us -> none  [the longest x4 6.24 us: collect(): lax.dot_general(onehot, parts[0], dims, preferred_element_type=jnp.float32)]
  transfers between devices with their start and end apart: 2 -> 0, of which waited for: 2 -> 0; matrix products, arithmetic and copies ran while one was open for 7% -> 0% of each run, Pallas kernels for 0% -> 0%
where the time goes in v2:
time: 88.2 us; the launch traced here: 88 us
  blocking collectives  61.8 us (70%)
  Pallas kernels  25.6 us (29%)
    all_to_all x1, blocking collectives, local(): x = lax.all_to_all(prep(0, tiles, own), 'bl', 0, 0, tiled=True)  43.1 us
    pallas_call x1, Pallas kernels, local(): call(functools.partial(main_kernel, dims, owned, groups), [(groups * part...  19.9 us
    all_to_all x1, blocking collectives, local(): held = lax.all_to_all(sent, ('chan', 'bl'), 0, 0, tiled=True)  18.7 us
    pallas_call x1, Pallas kernels, prep(): call(functools.partial(prep_kernel, dims), [(chans, count, LANE)], [HBM]...  3.97 us
    pallas_call x1, Pallas kernels, local(): call(functools.partial(finish_kernel, (directions, chans, owned, chans *...  1.78 us

profile of v2, /device:TPU:1, one launch (start us, length us, event | category | flops | bytes accessed | tf_op | source)
XLA Modules:
  0.0 88.0 jit_solution(17598299654513742852)
XLA Ops:
  0.6 4.0 %shard_map.103 = f32[16,336,128]{2,1,0:T(8,128)} custom-call(f32[2,16,2048]{2,1,0:T(8,128)} %vis_hbm.1, f32[256,2048]{1,0:T(8,128)} %bitcast.21, s32[2,2048]{1,0:T(2,128)} %pairs_hbm.1, f32[256,32]{1,0:T(8,128)} %bitcast.22, f32[256,32]{1,0:T(8,128)} %bitcast.23, f32[256,32]{1,0:T(8,128)} %bitcast.19), custom_call_target="tpu_custom_call" | custom-call | tf_op jit(solution)/shard_map/pallas_call | solution.py:343
  4.6 0.0 copy-start.2
  4.6 43.1 %all_to_all.10.x_ref = f32[16,336,128]{2,1,0:T(8,128)S(1)} all-to-all(f32[16,336,128]{2,1,0:T(8,128)} %shard_map.103), channel_id=1, replica_groups=mesh['chan'=8,'bl'=16] {'bl'}, dimensions={0} | all-to-all | bytes 5505024 | tf_op jit(solution)/shard_map/all_to_all | solution.py:351
  47.7 0.0 copy-done.2
  47.7 0.0 copy-start
  47.7 0.0 copy-start.1
  47.7 19.9 %shard_map.104 = f32[128,4,128]{2,1,0:T(4,128)S(1)} custom-call(f32[8]{0:T(128)S(1)} %copy-done.2, f32[16,336,128]{2,1,0:T(8,128)S(1)} %all_to_all.10.x_ref), custom_call_target="tpu_custom_call" | custom-call | tf_op jit(solution)/shard_map/pallas_call | solution.py:353
  67.6 18.7 %all_to_all.11.x_ref = f32[128,4,128]{2,1,0:T(4,128)S(1)} all-to-all(f32[128,4,128]{2,1,0:T(4,128)S(1)} %shard_map.104), channel_id=1, replica_groups=mesh['chan'=8,'bl'=16] {'chan','bl'}, dimensions={0} | all-to-all | bytes 524288 | tf_op jit(solution)/shard_map/all_to_all | solution.py:364
  86.3 0.0 copy-done
  86.3 0.0 copy-done.1
  86.3 1.8 %shard_map.105 = (f32[256,32]{1,0:T(8,128)}, f32[256,32]{1,0:T(8,128)}, f32[256,32]{1,0:T(8,128)}) custom-call(f32[8]{0:T(128)S(1)} %copy-done.2, f32[512]{0:T(512)S(1)} %copy-done.1, f32[128,4,128]{2,1,0:T(4,128)S(1)} %all_to_all.11.x_ref, f32[256,32]{1,0:T(8,128)S(1)} %bitcast.20), custom_call_target="tpu_custom_call" | custom-call | tf_op jit(solution)/shard_map/pallas_call | solution.py:365
Async XLA Ops:
  4.6 43.1 %copy-start.2 = (f32[8]{0:T(128)S(1)}, f32[8]{0:T(128)}, u32[]{:S(2)}) copy-start(f32[8]{0:T(128)} %penalty_ref.3) | copy-start | bytes 100
  47.7 38.6 %copy-start = (f32[32,2,8,16]{0,3,2,1:T(8,128)S(1)}, f32[32,2,8,16]{0,3,2,1:T(8,128)}, u32[]{:S(2)}) copy-start(f32[32,2,8,16]{0,3,2,1:T(8,128)} %param.13) | copy-start | bytes 98308
  47.7 38.6 %copy-start.1 = (f32[512]{0:T(512)S(1)}, f32[512]{0:T(512)}, u32[]{:S(2)}) copy-start(f32[512]{0:T(512)} %constant.2.clone.basis_ref) | copy-start | bytes 6148

commit v3 on v2

--- a/solution.py
+++ b/solution.py
@@ -12,7 +12,7 @@
 POLY = 4
 LANE = 128
 GROUP = 1
-UNROLL = 4
+UNROLL = 8
 VMEM = pl.BlockSpec(memory_space=pltpu.VMEM)
 SMEM = pl.BlockSpec(memory_space=pltpu.SMEM)
 HBM = pl.BlockSpec(memory_space=pltpu.HBM)
@@ -30,21 +30,34 @@
     return np.stack(columns, axis=1).astype(np.float32)
 
 
-def prep_kernel(dims, vis_hbm, coh_hbm, pairs_hbm, *rest):
-    directions, chans, start, tiles, owned, with_own = dims
-    if with_own:
-        gain_hbm, cons_hbm, dual_hbm, out_ref, coh_scr, vis_scr, pairs_scr, sems, own_scr, all_scr = rest
-    else:
-        out_ref, coh_scr, vis_scr, pairs_scr, sems = rest
-    base = tiles * 2 * directions
+def prep_kernel(
+    dims,
+    vis_hbm,
+    coh_hbm,
+    pairs_hbm,
+    gain_hbm,
+    cons_hbm,
+    dual_hbm,
+    out_hbm,
+    coh_scr,
+    vis_scr,
+    pairs_scr,
+    own_scr,
+    all_scr,
+    out_scr,
+    sems,
+    out_sems,
+):
+    directions, chans, tiles, owned = dims
+    depth = 2 * directions
+    base = tiles * depth
     copies = [pltpu.make_async_copy(pairs_hbm, pairs_scr, sems.at[2 * tiles])]
-    if with_own:
-        for i, ref in enumerate((gain_hbm, cons_hbm, dual_hbm)):
-            copies.append(pltpu.make_async_copy(ref, own_scr.at[i], sems.at[2 * tiles + 1 + i]))
+    for i, ref in enumerate((gain_hbm, cons_hbm, dual_hbm)):
+        copies.append(pltpu.make_async_copy(ref, own_scr.at[i], sems.at[2 * tiles + 1 + i]))
     vis_copies = []
     coh_copies = []
     for tile in range(tiles):
-        cut = pl.ds((start + tile) * LANE, LANE)
+        cut = pl.ds(tile * LANE, LANE)
         coh_copies.append(
             pltpu.make_async_copy(coh_hbm.at[:, cut], coh_scr.at[tile], sems.at[tile])
         )
@@ -59,32 +72,47 @@
         copy.start()
     for copy in copies:
         copy.wait()
-    if with_own:
-        own = [own_scr[i] for i in range(3)]
-        all_scr[...] = jnp.concatenate(own + [jnp.zeros_like(own[0])], axis=1)
-        for chan in range(chans):
-            rows = pl.ds(chan, 2 * directions, stride=chans)
-            out_ref[chan, pl.ds(base + 4 * tiles, 2 * directions)] = all_scr[rows, :]
-    for tile in range(tiles):
-        for side in range(2):
-            row = pairs_scr[side : side + 1, pl.ds((start + tile) * LANE, LANE)]
-            row = row.astype(jnp.float32)
-            for chan in range(chans):
-                out_ref[chan, pl.ds(base + (2 + side) * tiles + tile, 1)] = row
+    own = [own_scr[i] for i in range(3)]
+    all_scr[...] = jnp.concatenate(own + [jnp.zeros_like(own[0])], axis=1)
+    for chan in range(chans):
+        rows = pl.ds(chan, depth, stride=chans)
+        out_scr[chan, pl.ds(base + 4 * tiles, depth)] = all_scr[rows, :]
+    for side in range(2):
+        for tile in range(tiles):
+            row = pairs_scr[side : side + 1, pl.ds(tile * LANE, LANE)].astype(jnp.float32)
+            all_scr[pl.ds(side * tiles + tile, 1), :] = row
+    pairs = all_scr[pl.ds(0, 2 * tiles)]
+    for chan in range(chans):
+        out_scr[chan, pl.ds(base + 2 * tiles, 2 * tiles)] = pairs
+    out_copies = []
+
+    def send(first, rows):
+        cut = pl.ds(first, rows)
+        copy = pltpu.make_async_copy(
+            out_scr.at[:, cut], out_hbm.at[:, cut], out_sems.at[len(out_copies)]
+        )
+        copy.start()
+        out_copies.append(copy)
+
     for tile in range(tiles):
         coh_copies[tile].wait()
         for chan in range(chans):
             for part in range(2):
-                out_ref[chan, pl.ds((2 * tile + part) * directions, directions)] = coh_scr[
+                out_scr[chan, pl.ds((2 * tile + part) * directions, directions)] = coh_scr[
                     tile, pl.ds(part * directions * chans + chan, directions, stride=chans)
                 ]
+        if tile % 2:
+            send((tile - 1) * depth, 2 * depth)
     for copy in vis_copies:
         copy.wait()
     for chan in range(chans):
         for part in range(2):
-            out_ref[chan, pl.ds(base + part * tiles, tiles)] = vis_scr[
+            out_scr[chan, pl.ds(base + part * tiles, tiles)] = vis_scr[
                 part, pl.ds(chan, tiles, stride=chans)
             ]
+    send(base, 4 * tiles + depth)
+    for copy in out_copies:
+        copy.wait()
 
 
 def pick(tables, low, highs):
@@ -113,21 +141,25 @@
 
 
 class Sweep:
-    def __init__(self, dims, x_ref, pair_scr, sums_scr):
+    def __init__(self, dims, x_ref, pair_scr, float_scr, sums_scr):
         self.directions, self.tiles, self.stations, self.parts = dims
-        self.x_ref, self.pair_scr, self.sums_scr = x_ref, pair_scr, sums_scr
+        self.x_ref, self.sums_scr = x_ref, sums_scr
+        self.pair_scr, self.float_scr = pair_scr, float_scr
         self.first = self.tiles * 2 * self.directions
 
     def index(self):
         tiles = self.tiles
         for part in range(self.parts):
             whole = self.x_ref[part, pl.ds(self.first + 2 * tiles, 2 * tiles)].astype(jnp.int32)
-            self.pair_scr[part, pl.ds(0, 2 * tiles)] = jnp.bitwise_and(whole, LANE - 1)
-            self.pair_scr[part, pl.ds(2 * tiles, 2 * tiles)] = jnp.right_shift(whole, 7)
+            low, high = jnp.bitwise_and(whole, LANE - 1), jnp.right_shift(whole, 7)
+            self.pair_scr[part, pl.ds(0, 2 * tiles)] = low
+            self.pair_scr[part, pl.ds(2 * tiles, 2 * tiles)] = high
+            self.float_scr[part, pl.ds(0, 2 * tiles)] = low.astype(jnp.float32)
+            self.float_scr[part, pl.ds(2 * tiles, 2 * tiles)] = high.astype(jnp.float32)
 
     def fill(self, part, tables):
         directions, tiles, first = self.directions, self.tiles, self.first
-        x_ref, pair_scr = self.x_ref, self.pair_scr
+        x_ref, pair_scr, float_scr = self.x_ref, self.pair_scr, self.float_scr
         stripes = self.stations // LANE
         depth = 6 * directions
         wide = (LANE // 16, 16, LANE)
@@ -135,11 +167,11 @@
         labels = labels.astype(jnp.bfloat16).reshape(wide)
         one, zero = jnp.ones(wide, jnp.bfloat16), jnp.zeros(wide, jnp.bfloat16)
 
-        def twice(rows):
-            return jnp.concatenate([rows, rows], axis=0).astype(jnp.bfloat16)
-
-        def rows16(row):
-            return jnp.broadcast_to(row.astype(jnp.float32), (16, LANE)).astype(jnp.bfloat16)
+        blank = jnp.zeros((16, LANE), jnp.bfloat16)
+
+        def rows16(at):
+            row = float_scr[part, pl.ds(at, 1)]
+            return jnp.broadcast_to(row, (16, LANE)).astype(jnp.bfloat16)
 
         lefts, rights = [], []
         for tile in range(tiles):
@@ -152,8 +184,9 @@
                 high8 = jnp.broadcast_to(high, (directions, LANE))
                 highs = [high8 == s for s in range(stripes)]
                 gains.append([pick(tables[j], low8, highs) for j in range(2)])
-                masks.append([twice(jnp.where(h, 1.0, 0.0)) for h in highs])
-                hot = jnp.where(labels == rows16(low)[None], one, zero)
+                high16 = rows16((2 + side) * tiles + tile)
+                masks.append([high16 == jnp.bfloat16(s) for s in range(stripes)])
+                hot = jnp.where(labels == rows16(side * tiles + tile)[None], one, zero)
                 rights.append(hot.reshape(LANE, LANE))
             (gp_re, gp_im), (gq_re, gq_im) = gains
             coh_re, coh_im = [
@@ -181,12 +214,12 @@
                 power * (gp_re * gp_re + gp_im * gp_im),
             )
             for side, terms in enumerate((terms_p, terms_q)):
-                both = jnp.stack(terms)
                 lefts.append(
                     jnp.concatenate(
                         [
-                            (both * masks[side][s][None]).reshape(depth, LANE)
+                            jnp.where(masks[side][s], term, blank)
                             for s in range(stripes)
+                            for term in terms
                         ],
                         axis=0,
                     )
@@ -223,7 +256,8 @@
 
 
 def main_kernel(
-    dims, owned, groups, penalty_ref, x_ref, out_ref, table_scr, base_scr, pair_scr, sums_scr
+    dims, owned, groups, penalty_ref, x_ref, out_ref, table_scr, base_scr, pair_scr, float_scr,
+    sums_scr
 ):
     directions, tiles, stations, parts = dims
     stripes = stations // LANE
@@ -237,7 +271,7 @@
         table_scr[j] = gain[cut]
         base_scr[j] = mu * cons[cut] - 0.5 * dual[cut]
         base_scr[2 + j] = dual[cut] / rho
-    sweep = Sweep(dims, x_ref, pair_scr, sums_scr)
+    sweep = Sweep(dims, x_ref, pair_scr, float_scr, sums_scr)
     sweep.index()
 
     for gain_pass in range(PASSES):
@@ -328,27 +362,24 @@
     own = (flat(gains_start), flat(consensus_prev), flat(dual_prev))
     basis = jnp.asarray(poly_basis(chans * groups, POLY).reshape(-1))
 
-    def prep(start, span, own):
-        count = span * (2 * directions + 4) + (2 * directions if own else 0)
-        scratch = [
-            pltpu.VMEM((span, width, LANE), jnp.float32),
-            pltpu.VMEM((2, span * chans, LANE), jnp.float32),
+    count = tiles * (2 * directions + 4) + 2 * directions
+    packed = pl.pallas_call(
+        functools.partial(prep_kernel, (directions, chans, tiles, owned)),
+        out_shape=jax.ShapeDtypeStruct((chans, count, LANE), jnp.float32),
+        in_specs=[HBM] * 6,
+        out_specs=HBM,
+        scratch_shapes=[
+            pltpu.VMEM((tiles, width, LANE), jnp.float32),
+            pltpu.VMEM((2, tiles * chans, LANE), jnp.float32),
             pltpu.VMEM(station_pairs.shape, jnp.int32),
-            pltpu.SemaphoreType.DMA((2 * span + 4,)),
-        ]
-        if own:
-            scratch.append(pltpu.VMEM((3, width, owned), jnp.float32))
-            scratch.append(pltpu.VMEM((width, LANE), jnp.float32))
-        dims = (directions, chans, start, span, owned, bool(own))
-        return call(
-            functools.partial(prep_kernel, dims),
-            [(chans, count, LANE)],
-            [HBM] * (3 + len(own)),
-            limit=pltpu.CompilerParams(),
-            scratch_shapes=scratch,
-        )(visibilities, coherencies.reshape(width, lanes), station_pairs, *own)[0]
-
-    x = lax.all_to_all(prep(0, tiles, own), "bl", 0, 0, tiled=True)
+            pltpu.VMEM((3, width, owned), jnp.float32),
+            pltpu.VMEM((width, LANE), jnp.float32),
+            pltpu.VMEM((chans, count, LANE), jnp.float32),
+            pltpu.SemaphoreType.DMA((2 * tiles + 4,)),
+            pltpu.SemaphoreType.DMA((tiles // 2 + 1,)),
+        ],
+    )(visibilities, coherencies.reshape(width, lanes), station_pairs, *own)
+    x = lax.all_to_all(packed, "bl", 0, 0, tiled=True)
     dims = (directions, tiles, stations, parts)
     (sent,) = call(
         functools.partial(main_kernel, dims, owned, groups),
@@ -358,6 +389,7 @@
             pltpu.VMEM((2, directions, stations), jnp.float32),
             pltpu.VMEM((4, directions, stations), jnp.float32),
             pltpu.VMEM((parts, 4 * tiles, LANE), jnp.int32),
+            pltpu.VMEM((parts, 4 * tiles, LANE), jnp.float32),
             pltpu.VMEM((depth, LANE), jnp.float32),
         ],
     )(penalty, x)

time: 88.2 us -> 85.8 us (0.973)
  Pallas kernels: 25.6 us -> 23.1 us
    pallas_call x1, Pallas kernels: 19.9 us -> 18 us  [local(): call(functools.partial(main_kernel, dims, owned, groups), [(groups * part...]
where the time goes in v3:
time: 85.8 us; the launch traced here: 85.6 us
  blocking collectives  61.8 us (72%)
  Pallas kernels  23.1 us (27%)
    all_to_all x1, blocking collectives, local(): x = lax.all_to_all(packed, 'bl', 0, 0, tiled=True)  43.1 us
    all_to_all x1, blocking collectives, local(): held = lax.all_to_all(sent, ('chan', 'bl'), 0, 0, tiled=True)  18.7 us
    pallas_call x1, Pallas kernels, local(): call(functools.partial(main_kernel, dims, owned, groups), [(groups * part...  18 us
    pallas_call x1, Pallas kernels, local(): pl.pallas_call(functools.partial(prep_kernel, (directions, chans, tiles,...  3.32 us
    pallas_call x1, Pallas kernels, local(): call(functools.partial(finish_kernel, (directions, chans, owned, chans *...  1.78 us

profile of v3, /device:TPU:1, one launch (start us, length us, event | category | flops | bytes accessed | tf_op | source)
XLA Modules:
  0.0 85.6 jit_solution(3227782397502536619)
XLA Ops:
  0.6 3.3 %shard_map.103 = f32[16,336,128]{2,1,0:T(8,128)} custom-call(f32[2,16,2048]{2,1,0:T(8,128)} %vis_hbm.1, f32[256,2048]{1,0:T(8,128)} %bitcast.21, s32[2,2048]{1,0:T(2,128)} %pairs_hbm.1, f32[256,32]{1,0:T(8,128)} %bitcast.22, f32[256,32]{1,0:T(8,128)} %bitcast.23, f32[256,32]{1,0:T(8,128)} %bitcast.19), custom_call_target="tpu_custom_call" | custom-call | tf_op jit(solution)/shard_map/pallas_call | solution.py:366
  4.0 0.0 copy-start.2
  4.0 43.1 %all_to_all.10.x_ref = f32[16,336,128]{2,1,0:T(8,128)S(1)} all-to-all(f32[16,336,128]{2,1,0:T(8,128)} %shard_map.103), channel_id=1, replica_groups=mesh['chan'=8,'bl'=16] {'bl'}, dimensions={0} | all-to-all | bytes 5505024 | tf_op jit(solution)/shard_map/all_to_all | solution.py:382
  47.0 0.0 copy-done.2
  47.0 0.0 copy-start
  47.0 0.0 copy-start.1
  47.0 18.0 %shard_map.104 = f32[128,4,128]{2,1,0:T(4,128)S(1)} custom-call(f32[8]{0:T(128)S(1)} %copy-done.2, f32[16,336,128]{2,1,0:T(8,128)S(1)} %all_to_all.10.x_ref), custom_call_target="tpu_custom_call" | custom-call | tf_op jit(solution)/shard_map/pallas_call | solution.py:384
  65.1 18.7 %all_to_all.11.x_ref = f32[128,4,128]{2,1,0:T(4,128)S(1)} all-to-all(f32[128,4,128]{2,1,0:T(4,128)S(1)} %shard_map.104), channel_id=1, replica_groups=mesh['chan'=8,'bl'=16] {'chan','bl'}, dimensions={0} | all-to-all | bytes 524288 | tf_op jit(solution)/shard_map/all_to_all | solution.py:396
  83.8 0.0 copy-done
  83.8 0.0 copy-done.1
  83.8 1.8 %shard_map.105 = (f32[256,32]{1,0:T(8,128)}, f32[256,32]{1,0:T(8,128)}, f32[256,32]{1,0:T(8,128)}) custom-call(f32[8]{0:T(128)S(1)} %copy-done.2, f32[512]{0:T(512)S(1)} %copy-done.1, f32[128,4,128]{2,1,0:T(4,128)S(1)} %all_to_all.11.x_ref, f32[256,32]{1,0:T(8,128)S(1)} %bitcast.20), custom_call_target="tpu_custom_call" | custom-call | tf_op jit(solution)/shard_map/pallas_call | solution.py:397
Async XLA Ops:
  4.0 43.1 %copy-start.2 = (f32[8]{0:T(128)S(1)}, f32[8]{0:T(128)}, u32[]{:S(2)}) copy-start(f32[8]{0:T(128)} %penalty_ref.3) | copy-start | bytes 100
  47.0 36.8 %copy-start = (f32[32,2,8,16]{0,3,2,1:T(8,128)S(1)}, f32[32,2,8,16]{0,3,2,1:T(8,128)}, u32[]{:S(2)}) copy-start(f32[32,2,8,16]{0,3,2,1:T(8,128)} %param.13) | copy-start | bytes 98308
  47.0 36.8 %copy-start.1 = (f32[512]{0:T(512)S(1)}, f32[512]{0:T(512)}, u32[]{:S(2)}) copy-start(f32[512]{0:T(512)} %constant.2.clone.basis_ref) | copy-start | bytes 6148

commit v4 on v3

--- a/solution.py
+++ b/solution.py
@@ -41,6 +41,7 @@
     out_hbm,
     coh_scr,
     vis_scr,
+    vis_raw,
     pairs_scr,
     own_scr,
     all_scr,
@@ -51,24 +52,17 @@
     directions, chans, tiles, owned = dims
     depth = 2 * directions
     base = tiles * depth
-    copies = [pltpu.make_async_copy(pairs_hbm, pairs_scr, sems.at[2 * tiles])]
+    copies = [pltpu.make_async_copy(pairs_hbm, pairs_scr, sems.at[tiles])]
     for i, ref in enumerate((gain_hbm, cons_hbm, dual_hbm)):
-        copies.append(pltpu.make_async_copy(ref, own_scr.at[i], sems.at[2 * tiles + 1 + i]))
-    vis_copies = []
+        copies.append(pltpu.make_async_copy(ref, own_scr.at[i], sems.at[tiles + 1 + i]))
     coh_copies = []
     for tile in range(tiles):
         cut = pl.ds(tile * LANE, LANE)
         coh_copies.append(
             pltpu.make_async_copy(coh_hbm.at[:, cut], coh_scr.at[tile], sems.at[tile])
         )
-        vis_copies.append(
-            pltpu.make_async_copy(
-                vis_hbm.at[:, :, cut],
-                vis_scr.at[:, pl.ds(tile * chans, chans)],
-                sems.at[tiles + tile],
-            )
-        )
-    for copy in copies + coh_copies + vis_copies:
+    vis_copy = pltpu.make_async_copy(vis_hbm, vis_raw, sems.at[tiles + 4])
+    for copy in copies + coh_copies + [vis_copy]:
         copy.start()
     for copy in copies:
         copy.wait()
@@ -101,10 +95,12 @@
                 out_scr[chan, pl.ds((2 * tile + part) * directions, directions)] = coh_scr[
                     tile, pl.ds(part * directions * chans + chan, directions, stride=chans)
                 ]
-        if tile % 2:
-            send((tile - 1) * depth, 2 * depth)
-    for copy in vis_copies:
-        copy.wait()
+        if tile % 4 == 3:
+            send((tile - 3) * depth, 4 * depth)
+    vis_copy.wait()
+    for tile in range(tiles):
+        for part in range(2):
+            vis_scr[part, pl.ds(tile * chans, chans)] = vis_raw[part, :, pl.ds(tile * LANE, LANE)]
     for chan in range(chans):
         for part in range(2):
             out_scr[chan, pl.ds(base + part * tiles, tiles)] = vis_scr[
@@ -306,11 +302,12 @@
     directions, chans, owned, count = dims
     half = directions // 2
     start = lax.axis_index("chan") * chans
-    coefs = [jnp.zeros((half, LANE), jnp.float32) for _ in range(POLY)]
+    chains = [[jnp.zeros((half, LANE), jnp.float32)] * 4 for _ in range(POLY)]
     for channel in range(count):
         block = x_ref[channel]
         for m in range(POLY):
-            coefs[m] = coefs[m] + block * basis_ref[channel * POLY + m]
+            chains[m][channel % 4] += block * basis_ref[channel * POLY + m]
+    coefs = [(c[0] + c[1]) + (c[2] + c[3]) for c in chains]
     for chan in range(chans):
         block = x_ref[start + chan]
         cons = coefs[0] * basis_ref[(start + chan) * POLY]
@@ -371,12 +368,13 @@
         scratch_shapes=[
             pltpu.VMEM((tiles, width, LANE), jnp.float32),
             pltpu.VMEM((2, tiles * chans, LANE), jnp.float32),
+            pltpu.VMEM(visibilities.shape, jnp.float32),
             pltpu.VMEM(station_pairs.shape, jnp.int32),
             pltpu.VMEM((3, width, owned), jnp.float32),
             pltpu.VMEM((width, LANE), jnp.float32),
             pltpu.VMEM((chans, count, LANE), jnp.float32),
-            pltpu.SemaphoreType.DMA((2 * tiles + 4,)),
-            pltpu.SemaphoreType.DMA((tiles // 2 + 1,)),
+            pltpu.SemaphoreType.DMA((tiles + 5,)),
+            pltpu.SemaphoreType.DMA((tiles // 4 + 1,)),
         ],
     )(visibilities, coherencies.reshape(width, lanes), station_pairs, *own)
     x = lax.all_to_all(packed, "bl", 0, 0, tiled=True)

time: 85.8 us -> 85.7 us (level)
  no operation moved by 1% of the time
where the time goes in v4:
time: 85.7 us; the launch traced here: 85.5 us
  blocking collectives  61.8 us (72%)
  Pallas kernels  23.1 us (27%)
    all_to_all x1, blocking collectives, local(): x = lax.all_to_all(packed, 'bl', 0, 0, tiled=True)  43.1 us
    all_to_all x1, blocking collectives, local(): held = lax.all_to_all(sent, ('chan', 'bl'), 0, 0, tiled=True)  18.7 us
    pallas_call x1, Pallas kernels, local(): call(functools.partial(main_kernel, dims, owned, groups), [(groups * part...  18 us
    pallas_call x1, Pallas kernels, local(): pl.pallas_call(functools.partial(prep_kernel, (directions, chans, tiles,...  3.26 us
    pallas_call x1, Pallas kernels, local(): call(functools.partial(finish_kernel, (directions, chans, owned, chans *...  1.77 us

profile of v4, /device:TPU:1, one launch (start us, length us, event | category | flops | bytes accessed | tf_op | source)
XLA Modules:
  0.0 85.5 jit_solution(14645189767941955480)
XLA Ops:
  0.6 3.3 %shard_map.103 = f32[16,336,128]{2,1,0:T(8,128)} custom-call(f32[2,16,2048]{2,1,0:T(8,128)} %vis_hbm.1, f32[256,2048]{1,0:T(8,128)} %bitcast.21, s32[2,2048]{1,0:T(2,128)} %pairs_hbm.1, f32[256,32]{1,0:T(8,128)} %bitcast.22, f32[256,32]{1,0:T(8,128)} %bitcast.23, f32[256,32]{1,0:T(8,128)} %bitcast.19), custom_call_target="tpu_custom_call" | custom-call | tf_op jit(solution)/shard_map/pallas_call | solution.py:363
  3.9 0.0 copy-start.2
  3.9 43.1 %all_to_all.10.x_ref = f32[16,336,128]{2,1,0:T(8,128)S(1)} all-to-all(f32[16,336,128]{2,1,0:T(8,128)} %shard_map.103), channel_id=1, replica_groups=mesh['chan'=8,'bl'=16] {'bl'}, dimensions={0} | all-to-all | bytes 5505024 | tf_op jit(solution)/shard_map/all_to_all | solution.py:380
  47.0 0.0 copy-done.2
  47.0 0.0 copy-start
  47.0 0.0 copy-start.1
  47.0 18.0 %shard_map.104 = f32[128,4,128]{2,1,0:T(4,128)S(1)} custom-call(f32[8]{0:T(128)S(1)} %copy-done.2, f32[16,336,128]{2,1,0:T(8,128)S(1)} %all_to_all.10.x_ref), custom_call_target="tpu_custom_call" | custom-call | tf_op jit(solution)/shard_map/pallas_call | solution.py:382
  65.0 18.7 %all_to_all.11.x_ref = f32[128,4,128]{2,1,0:T(4,128)S(1)} all-to-all(f32[128,4,128]{2,1,0:T(4,128)S(1)} %shard_map.104), channel_id=1, replica_groups=mesh['chan'=8,'bl'=16] {'chan','bl'}, dimensions={0} | all-to-all | bytes 524288 | tf_op jit(solution)/shard_map/all_to_all | solution.py:394
  83.7 0.0 copy-done
  83.7 0.0 copy-done.1
  83.7 1.8 %shard_map.105 = (f32[256,32]{1,0:T(8,128)}, f32[256,32]{1,0:T(8,128)}, f32[256,32]{1,0:T(8,128)}) custom-call(f32[8]{0:T(128)S(1)} %copy-done.2, f32[512]{0:T(512)S(1)} %copy-done.1, f32[128,4,128]{2,1,0:T(4,128)S(1)} %all_to_all.11.x_ref, f32[256,32]{1,0:T(8,128)S(1)} %bitcast.20), custom_call_target="tpu_custom_call" | custom-call | tf_op jit(solution)/shard_map/pallas_call | solution.py:395
Async XLA Ops:
  3.9 43.1 %copy-start.2 = (f32[8]{0:T(128)S(1)}, f32[8]{0:T(128)}, u32[]{:S(2)}) copy-start(f32[8]{0:T(128)} %penalty_ref.3) | copy-start | bytes 100
  47.0 36.8 %copy-start = (f32[32,2,8,16]{0,3,2,1:T(8,128)S(1)}, f32[32,2,8,16]{0,3,2,1:T(8,128)}, u32[]{:S(2)}) copy-start(f32[32,2,8,16]{0,3,2,1:T(8,128)} %param.13) | copy-start | bytes 98308
  47.0 36.8 %copy-start.1 = (f32[512]{0:T(512)S(1)}, f32[512]{0:T(512)}, u32[]{:S(2)}) copy-start(f32[512]{0:T(512)} %constant.2.clone.basis_ref) | copy-start | bytes 6148

commit v5 on v4

--- a/solution.py
+++ b/solution.py
@@ -62,7 +62,7 @@
             pltpu.make_async_copy(coh_hbm.at[:, cut], coh_scr.at[tile], sems.at[tile])
         )
     vis_copy = pltpu.make_async_copy(vis_hbm, vis_raw, sems.at[tiles + 4])
-    for copy in copies + coh_copies + [vis_copy]:
+    for copy in copies + [vis_copy] + coh_copies:
         copy.start()
     for copy in copies:
         copy.wait()
@@ -88,15 +88,6 @@
         copy.start()
         out_copies.append(copy)
 
-    for tile in range(tiles):
-        coh_copies[tile].wait()
-        for chan in range(chans):
-            for part in range(2):
-                out_scr[chan, pl.ds((2 * tile + part) * directions, directions)] = coh_scr[
-                    tile, pl.ds(part * directions * chans + chan, directions, stride=chans)
-                ]
-        if tile % 4 == 3:
-            send((tile - 3) * depth, 4 * depth)
     vis_copy.wait()
     for tile in range(tiles):
         for part in range(2):
@@ -107,6 +98,15 @@
                 part, pl.ds(chan, tiles, stride=chans)
             ]
     send(base, 4 * tiles + depth)
+    for tile in range(tiles):
+        coh_copies[tile].wait()
+        for chan in range(chans):
+            for part in range(2):
+                out_scr[chan, pl.ds((2 * tile + part) * directions, directions)] = coh_scr[
+                    tile, pl.ds(part * directions * chans + chan, directions, stride=chans)
+                ]
+        if tile % 4 == 3:
+            send((tile - 3) * depth, 4 * depth)
     for copy in out_copies:
         copy.wait()
 

time: 85.7 us -> 85.6 us (level)
  no operation moved by 1% of the time
where the time goes in v5:
time: 85.6 us; the launch traced here: 85.3 us
  blocking collectives  61.8 us (72%)
  Pallas kernels  22.9 us (27%)
    all_to_all x1, blocking collectives, local(): x = lax.all_to_all(packed, 'bl', 0, 0, tiled=True)  43.1 us
    all_to_all x1, blocking collectives, local(): held = lax.all_to_all(sent, ('chan', 'bl'), 0, 0, tiled=True)  18.7 us
    pallas_call x1, Pallas kernels, local(): call(functools.partial(main_kernel, dims, owned, groups), [(groups * part...  18 us
    pallas_call x1, Pallas kernels, local(): pl.pallas_call(functools.partial(prep_kernel, (directions, chans, tiles,...  3.09 us
    pallas_call x1, Pallas kernels, local(): call(functools.partial(finish_kernel, (directions, chans, owned, chans *...  1.77 us

profile of v5, /device:TPU:1, one launch (start us, length us, event | category | flops | bytes accessed | tf_op | source)
XLA Modules:
  0.0 85.3 jit_solution(1158349940168932911)
XLA Ops:
  0.6 3.1 %shard_map.103 = f32[16,336,128]{2,1,0:T(8,128)} custom-call(f32[2,16,2048]{2,1,0:T(8,128)} %vis_hbm.1, f32[256,2048]{1,0:T(8,128)} %bitcast.21, s32[2,2048]{1,0:T(2,128)} %pairs_hbm.1, f32[256,32]{1,0:T(8,128)} %bitcast.22, f32[256,32]{1,0:T(8,128)} %bitcast.23, f32[256,32]{1,0:T(8,128)} %bitcast.19), custom_call_target="tpu_custom_call" | custom-call | tf_op jit(solution)/shard_map/pallas_call | solution.py:363
  3.7 0.0 copy-start.2
  3.7 43.1 %all_to_all.10.x_ref = f32[16,336,128]{2,1,0:T(8,128)S(1)} all-to-all(f32[16,336,128]{2,1,0:T(8,128)} %shard_map.103), channel_id=1, replica_groups=mesh['chan'=8,'bl'=16] {'bl'}, dimensions={0} | all-to-all | bytes 5505024 | tf_op jit(solution)/shard_map/all_to_all | solution.py:380
  46.8 0.0 copy-done.2
  46.8 0.0 copy-start
  46.8 0.0 copy-start.1
  46.8 18.0 %shard_map.104 = f32[128,4,128]{2,1,0:T(4,128)S(1)} custom-call(f32[8]{0:T(128)S(1)} %copy-done.2, f32[16,336,128]{2,1,0:T(8,128)S(1)} %all_to_all.10.x_ref), custom_call_target="tpu_custom_call" | custom-call | tf_op jit(solution)/shard_map/pallas_call | solution.py:382
  64.9 18.7 %all_to_all.11.x_ref = f32[128,4,128]{2,1,0:T(4,128)S(1)} all-to-all(f32[128,4,128]{2,1,0:T(4,128)S(1)} %shard_map.104), channel_id=1, replica_groups=mesh['chan'=8,'bl'=16] {'chan','bl'}, dimensions={0} | all-to-all | bytes 524288 | tf_op jit(solution)/shard_map/all_to_all | solution.py:394
  83.6 0.0 copy-done
  83.6 0.0 copy-done.1
  83.6 1.8 %shard_map.105 = (f32[256,32]{1,0:T(8,128)}, f32[256,32]{1,0:T(8,128)}, f32[256,32]{1,0:T(8,128)}) custom-call(f32[8]{0:T(128)S(1)} %copy-done.2, f32[512]{0:T(512)S(1)} %copy-done.1, f32[128,4,128]{2,1,0:T(4,128)S(1)} %all_to_all.11.x_ref, f32[256,32]{1,0:T(8,128)S(1)} %bitcast.20), custom_call_target="tpu_custom_call" | custom-call | tf_op jit(solution)/shard_map/pallas_call | solution.py:395
Async XLA Ops:
  3.7 43.1 %copy-start.2 = (f32[8]{0:T(128)S(1)}, f32[8]{0:T(128)}, u32[]{:S(2)}) copy-start(f32[8]{0:T(128)} %penalty_ref.3) | copy-start | bytes 100
  46.8 36.8 %copy-start = (f32[32,2,8,16]{0,3,2,1:T(8,128)S(1)}, f32[32,2,8,16]{0,3,2,1:T(8,128)}, u32[]{:S(2)}) copy-start(f32[32,2,8,16]{0,3,2,1:T(8,128)} %param.13) | copy-start | bytes 98308
  46.8 36.8 %copy-start.1 = (f32[512]{0:T(512)S(1)}, f32[512]{0:T(512)}, u32[]{:S(2)}) copy-start(f32[512]{0:T(512)} %constant.2.clone.basis_ref) | copy-start | bytes 6148
